TPU v7x, 32 devices: a whole 2x2x4 slice. The times are simulated.
32 devices in a mesh: groups: 2 (over x), right: 4 (over y, core), left: 4 (over z).
Axes of the slice: x: 2, y: 2, z: 4, core: 2. Of those that a mesh axis runs over, the one named last changes fastest.
Arguments:
- left_act: bfloat16 [4096, 8192], P(('groups', 'right'), 'left'), parts along dimension 0, may hold values from -15 to 15
- right_act: bfloat16 [4096, 4096], P(('groups', 'left'), 'right'), parts along dimension 0, may hold values from -15 to 15
- counts: int32 [512, 128], P(('groups', 'left'), 'right'), parts along dimension 0, may hold values from 512 to 2048
- w_out: bfloat16 [1024, 128], replicated, may hold values from -0.1875 to 0.1875
Outputs:
- pair_update: float32 [512, 128, 128], P(('groups', 'left'), 'right'), parts along dimension 0
There are 2 independent parts, one for each index of `groups`. A program takes and returns all parts, laid end to end along the dimension named above; an argument that names none is the same for every part. Nothing has to cross between parts.
All inputs are finite; a program needn't handle non-finite values.
Results may differ from a plain program's by a relative error of at most 0.0029.
Values may be sent and summed in bfloat16 or wider, within the bound.
No kernel may reach another device: no remote copies, remote signals or barrier semaphores. Data moves between devices by JAX's collectives and lax.ppermute only.
A program may use at most 128 MiB of HBM per device.

v0:
```python
import jax
import jax.numpy as jnp
from jax import lax
from jax.sharding import PartitionSpec as P

CH = 32


def contract_rows(first, second):
    return lax.dot_general(
        first, second, (((0,), (0,)), ((), ())), preferred_element_type=jnp.float32
    )


def shards(left_act, right_act, counts, w_out):
    left_dev = counts.shape[0]
    right_dev = counts.shape[1]
    left_full = lax.all_gather(left_act, "right", axis=0, tiled=True)
    outer = contract_rows(left_full, lax.all_gather(right_act, "left", axis=0, tiled=True))
    flat = (
        outer.reshape(left_dev, CH, right_dev, CH)
        .transpose(0, 2, 1, 3)
        .reshape(left_dev * right_dev, CH * CH)
    )
    flat = flat.astype(jnp.bfloat16)
    projected = jnp.dot(flat, w_out, preferred_element_type=jnp.float32).reshape(
        left_dev, right_dev, w_out.shape[1]
    )
    return projected / counts.astype(jnp.float32)[:, :, None]


def solution(mesh):
    in_specs = (
        P(("groups", "right"), "left"),
        P(("groups", "left"), "right"),
        P(("groups", "left"), "right"),
        P(),
    )
    out_specs = P(("groups", "left"), "right", None)
    return jax.shard_map(shards, mesh=mesh, in_specs=in_specs, out_specs=out_specs, check_vma=False)
```

profile of v0, /device:TPU:0, one launch (start us, length us, event | category | flops | bytes accessed | tf_op | source)
XLA Modules:
  0.0 221.0 jit_solution(8785365857728057451)
XLA Ops:
  6.5 0.0 copy-start
  6.5 0.0 all-gather.5.cloned.1.call-start
  6.5 0.7 all-gather.5.cloned.1.call-update
  7.3 0.0 all-gather.3.cloned.1.call-start
  7.3 0.7 all-gather.3.cloned.1.call-update
  8.0 0.7 convert_element_type.20
  8.7 0.1 copy.9
  8.8 83.6 %all-gather.5.cloned.1.call-done = bf16[2048,1024]{1,0:T(8,128)(2,1)} async-done(((bf16[512,1024]{1,0:T(8,128)(2,1)}), bf16[2048,1024]{1,0:T(8,128)(2,1)}) %all-gather.5.cloned.1.call-update) | async-done | bytes 4194320 | tf_op jit(solution)/shard_map/all_gather | solution.py:19
  92.4 58.4 %all-gather.3.cloned.1.call-done = bf16[2048,2048]{1,0:T(8,128)(2,1)} async-done(((bf16[512,2048]{1,0:T(8,128)(2,1)}), bf16[2048,2048]{1,0:T(8,128)(2,1)}) %all-gather.3.cloned.1.call-update) | async-done | bytes 8388624 | tf_op jit(solution)/shard_map/all_gather | solution.py:18
  150.8 14.0 %convolution_convert_fusion = bf16[2048,1024]{1,0:T(8,128)(2,1)} fusion(bf16[2048,2048]{1,0:T(8,128)(2,1)} %all-gather.3.cloned.1.call-done, bf16[2048,1024]{1,0:T(8,128)(2,1)} %all-gather.5.cloned.1.call-done), kind=kOutput, calls=%fused_computation | convolution fusion | flops 8592031744 | bytes 16777216 | tf_op jit(solution)/shard_map/dot_general | solution.py:10
  164.8 20.3 %convert_element_type.17 = bf16[64,32,32,32]{3,2,1,0:T(8,128)(2,1)} reshape(bf16[2048,1024]{1,0:T(8,128)(2,1)} %convolution_convert_fusion) | data formatting | bytes 8388608 | tf_op jit(solution)/shard_map/convert_element_type | solution.py:25
  185.1 21.7 %copy.7 = bf16[64,32,32,32]{0,3,2,1:T(8,128)(2,1)} copy(bf16[64,32,32,32]{3,1,2,0:T(8,128)(2,1)} %bitcast.8) | data formatting | bytes 8388608 | tf_op jit(solution)/shard_map/convert_element_type | solution.py:25
  206.8 0.0 copy-done
  206.8 5.7 %fusion = f32[64,32,128]{2,0,1:T(8,128)S(1)} fusion(bf16[64,32,1024]{0,2,1:T(8,128)(2,1)} %bitcast.9, bf16[1024,128]{1,0:T(8,128)(2,1)S(1)} %copy-done), kind=kOutput, calls=%fused_computation.2 | convolution fusion | flops 536870912 | bytes 5505024 | tf_op jit(solution)/shard_map/dot_general | solution.py:26
  212.5 1.7 copy_divide_fusion
Async XLA Ops:
  6.5 200.3 %copy-start = (bf16[1024,128]{1,0:T(8,128)(2,1)S(1)}, bf16[1024,128]{1,0:T(8,128)(2,1)}, u32[]{:S(2)}) copy-start(bf16[1024,128]{1,0:T(8,128)(2,1)} %param.7) | copy-start | bytes 786436
  6.5 85.9 %all-gather.5.cloned.1.call-start = ((), (), s32[]{:S(2)}) async-start(), calls=%async_computation.1 | async-start | bytes 5242880 | tf_op jit(solution)/shard_map/all_gather | solution.py:19
  7.3 143.6 %all-gather.3.cloned.1.call-start = ((), (), s32[]{:S(2)}) async-start(), calls=%async_computation | async-start | bytes 10485760 | tf_op jit(solution)/shard_map/all_gather | solution.py:18
Sparse Core Ops, SparseCore 0:
  8.9 83.4 all-gather.4
  94.0 56.8 all-gather.2
where the time goes:
time: 222 us; the launch traced here: 221 us
  waiting for transfers between devices  143 us (64%)
  local copies, waits for them, and re-layouts  42.1 us (19%)
  matrix products  19.7 us (9%)
  between operations  13.4 us (6%)
  other arithmetic  2.38 us (1%)
    all_gather x1, waiting for transfers between devices, shards(): lax.all_gather(right_act, 'left', axis=0, tiled=True)  83.6 us
    all_gather x1, waiting for transfers between devices, shards(): left_full = lax.all_gather(left_act, 'right', axis=0, tiled=True)  58.4 us
    convert_element_type x2, local copies, waits for them, and re-layouts, shards(): flat = flat.astype(jnp.bfloat16)  42 us
    dot_general x1, matrix products, contract_rows(): lax.dot_general(first, second, (((0,), (0,)), ((), ())), preferred_elemen...  14 us
    dot_general x1, matrix products, shards(): jnp.dot(flat, w_out, preferred_element_type=jnp.float32)  5.75 us
  transfers between devices with their start and end apart: 2, of which 2 were waited for; matrix products, arithmetic and copies ran while one was open for 0% of the time, Pallas kernels for 0%

commit v1 on v0

v1 whole, which is shorter than its diff:
```python
import functools

import jax
import jax.numpy as jnp
from jax import lax
from jax.experimental import pallas as pl
from jax.experimental.pallas import tpu as pltpu
from jax.sharding import PartitionSpec as P

CH = 32
LANES = 128
GROUP = LANES // CH
CORES = 2
PARTS = 2


def spread_weights(w_out):
    pair = w_out.shape[1]
    by_e = w_out.reshape(CH, CH, pair).transpose(1, 0, 2)
    same = jnp.eye(GROUP, dtype=jnp.bool_)[None, :, None, :, None]
    full = jnp.where(same, by_e[:, None, :, None, :], jnp.zeros((), w_out.dtype))
    return full.reshape(CH * LANES, GROUP * pair)


def kernel(line, nl, nr, part, *refs):
    left_refs, right_refs = refs[:nl], refs[nl : nl + nr]
    wide_ref, counts_ref = refs[nl + nr : nl + nr + 2]
    out_ref, left_v, right_v, rt, lhs, wide_v, counts_v, out_v, left_sem, right_sem, misc_sem = refs[-11:]
    seqs, width = left_v.shape
    cols = right_v.shape[1]
    res = cols // CH
    lrows = left_refs[0].shape[0]
    rrows = right_refs[0].shape[0]
    if line:
        l, r = lax.axis_index("left"), lax.axis_index("right")
        low = l < 2
        end = jnp.logical_or(l == 0, l == 3)

        def slot(s):
            return jnp.where(s // 2 == l // 2, (s + l) % 2, jnp.where(low, s, 3 - s))

        flip = r % 2
        near = r + 1 - 2 * flip
        far = (r + 2) % 4
        owners = (r, near, far, far + 1 - 2 * flip)
        places = [slot(s) for s in owners]
    else:
        places = [0]

    for b, place in enumerate(places):
        pltpu.make_async_copy(
            left_refs[b], left_v.at[pl.ds(pl.multiple_of(place * lrows, lrows), lrows), :], left_sem.at[b]
        ).start()

    def right_copy(src, b):
        return pltpu.make_async_copy(src, right_v.at[pl.ds(b * rrows, rrows), :], right_sem.at[b])

    if line:
        own, first, mid_a, end_a, mid_b, end_b = right_refs
        right_copy(own, 0).start()
        right_copy(first, 1).start()
        for b, at_mid, at_end in ((2, mid_a, end_a), (3, mid_b, end_b)):

            @pl.when(end)
            def _():
                right_copy(at_end, b).start()

            @pl.when(jnp.logical_not(end))
            def _():
                right_copy(at_mid, b).start()
    else:
        right_copy(right_refs[0], 0).start()
    wide_copy = pltpu.make_async_copy(wide_ref, wide_v, misc_sem.at[0])
    wide_copy.start()
    counts_copy = pltpu.make_async_copy(counts_ref, counts_v, misc_sem.at[1])
    counts_copy.start()

    to = lax.broadcasted_iota(jnp.int32, (cols, cols), 0)
    source = lax.broadcasted_iota(jnp.int32, (cols, cols), 1)
    perm = jnp.where(source == (to % res) * CH + to // res, 1.0, 0.0).astype(jnp.bfloat16)
    for b in range(seqs // rrows):
        right_copy(right_refs[0], b).wait()
        rows = pl.ds(b * rrows, rrows)
        rt[:, rows] = lax.dot_general(
            perm, right_v[rows, :], (((1,), (1,)), ((), ())), preferred_element_type=jnp.float32
        ).astype(jnp.bfloat16)
    for b in range(nl):
        pltpu.make_async_copy(left_refs[b], left_v.at[pl.ds(b * lrows, lrows), :], left_sem.at[b]).wait()
    outer = jnp.dot(rt[...], left_v[...], preferred_element_type=jnp.float32).astype(jnp.bfloat16)
    for g in range(width // LANES):
        for e in range(CH):
            lhs[g * res : (g + 1) * res, e * LANES : (e + 1) * LANES] = outer[
                e * res : (e + 1) * res, g * LANES : (g + 1) * LANES
            ]
    wide_copy.wait()
    counts_copy.wait()
    projected = jnp.dot(lhs[...], wide_v[...], preferred_element_type=jnp.float32)
    pair = out_v.shape[2]
    for g in range(width // LANES):
        for i in range(GROUP):
            row = g * GROUP + i
            out_v[row] = projected[g * res : (g + 1) * res, i * pair : (i + 1) * pair] / counts_v[:, row : row + 1]
    out_copy = pltpu.make_async_copy(out_v, out_ref.at[:, pl.ds(part * res, res), :], misc_sem.at[2])
    out_copy.start()
    out_copy.wait()


def pair_features(line, part, lefts, rights, wide, counts, right_dev, before):
    nl, nr = len(lefts), len(rights)
    seqs = lefts[0].shape[0] * nl
    width = lefts[0].shape[1]
    cols = rights[0].shape[1]
    res, left_dev = cols // CH, width // CH
    pair = wide.shape[1] // GROUP
    any_space = pl.BlockSpec(memory_space=pl.ANY)
    operands = [*lefts, *rights, wide, counts]
    aliases = {}
    if before is not None:
        aliases = {len(operands): 0}
        operands.append(before)
    return pl.pallas_call(
        functools.partial(kernel, line, nl, nr, part),
        out_shape=jax.ShapeDtypeStruct((left_dev, right_dev, pair), jnp.float32),
        in_specs=[any_space] * len(operands),
        out_specs=any_space,
        input_output_aliases=aliases,
        scratch_shapes=[
            pltpu.VMEM((seqs, width), jnp.bfloat16),
            pltpu.VMEM((seqs, cols), jnp.bfloat16),
            pltpu.VMEM((cols, seqs), jnp.bfloat16),
            pltpu.VMEM((width // LANES * res, CH * LANES), jnp.bfloat16),
            pltpu.VMEM(wide.shape, jnp.bfloat16),
            pltpu.VMEM(counts.shape, jnp.float32),
            pltpu.VMEM((left_dev, res, pair), jnp.float32),
            pltpu.SemaphoreType.DMA((nl,)),
            pltpu.SemaphoreType.DMA((4,)),
            pltpu.SemaphoreType.DMA((3,)),
        ],
        compiler_params=pltpu.CompilerParams(vmem_limit_bytes=48 * 2**20),
        cost_estimate=pl.CostEstimate(
            flops=2 * seqs * width * cols, bytes_accessed=2 * seqs * (width + cols), transcendentals=0
        ),
    )(*operands)


def tied(*values):
    return lax.optimization_barrier(values)


def gather_line(left_act, right_act):
    ends = ((0, 1), (1, 0), (2, 3), (3, 2))
    middle = ((1, 2), (2, 1))
    outward = ((1, 0), (2, 3))

    def hop(x, pairs):
        return lax.ppermute(x, "left", pairs)

    def partner(x, step):
        return lax.ppermute(x, "right", [(i, i ^ step) for i in range(4)])

    a, c = jnp.split(right_act, PARTS, axis=1)
    a1, a2 = hop(a, ends), hop(a, middle)
    far = partner(left_act, CORES)
    near = partner(left_act, 1)
    c1, c2 = hop(c, ends), hop(c, middle)
    a1, a2 = tied(a1, a2)
    a3, a4 = hop(a2, outward), hop(a1, middle)
    c1, c2 = tied(c1, c2)
    c3, c4 = hop(c2, outward), hop(c1, middle)
    a3, a4 = tied(a3, a4)
    a5 = hop(a4, outward)
    c3, c4 = tied(c3, c4)
    c5 = hop(c4, outward)
    cross = partner(far, 1)
    return [left_act, near, far, cross], [(a, a1, a2, a3, a4, a5), (c, c1, c2, c3, c4, c5)]


def shards(line, left_act, right_act, counts, w_out):
    if line:
        lefts, rights = gather_line(left_act, right_act)
    else:
        lefts = [lax.all_gather(left_act, "right", axis=0, tiled=True)]
        full = lax.all_gather(right_act, "left", axis=0, tiled=True)
        rights = [(x,) for x in jnp.split(full, PARTS, axis=1)]
    wide = spread_weights(w_out)
    by_right = jnp.split(counts.astype(jnp.float32).T, PARTS, axis=0)
    out = None
    for part in range(PARTS):
        out = pair_features(line, part, lefts, rights[part], wide, by_right[part], counts.shape[1], out)
    return out


def solution(mesh):
    in_specs = (
        P(("groups", "right"), "left"),
        P(("groups", "left"), "right"),
        P(("groups", "left"), "right"),
        P(),
    )
    out_specs = P(("groups", "left"), "right", None)
    line = mesh.shape["left"] == 4 and mesh.shape["right"] == 4
    body = functools.partial(shards, line)
    return jax.shard_map(body, mesh=mesh, in_specs=in_specs, out_specs=out_specs, check_vma=False)
```

time: 222 us -> 113 us (0.51)
  waiting for transfers between devices: 143 us -> 67.4 us
  local copies, waits for them, and re-layouts: 42.1 us -> 7.12 us
  matrix products: 19.7 us -> 0 us
  Pallas kernels: 0 us -> 19.3 us
  starting transfers between devices: 0.04 us -> 17 us
  between operations: 13.4 us -> 0.34 us
    all_gather x2 -> x0, waiting for transfers between devices: 142 us -> none  [the longest x1 83.6 us: shards(): lax.all_gather(right_act, 'left', axis=0, tiled=True)]
    ppermute x0 -> x13, waiting for transfers between devices: none -> 67.4 us  [the longest x3 37.8 us: partner(): return lax.ppermute(x, 'right', [(i, i ^ step) for i in range(4)])]
    convert_element_type x3 -> x0, local copies, waits for them, and re-layouts: 42.1 us -> none  [the longest x2 42 us: shards(): flat = flat.astype(jnp.bfloat16)]
    dot_general x2 -> x0, matrix products: 19.7 us -> none  [the longest x1 14 us: contract_rows(): lax.dot_general(first, second, (((0,), (0,)), ((), ())), preferred_elemen...]
    pallas_call x0 -> x2, Pallas kernels: none -> 19.3 us  [pair_features(): pl.pallas_call(functools.partial(kernel, line, nl, nr, part), out_shape=j...]
    ppermute x0 -> x13, starting transfers between devices: none -> 17 us  [the longest x10 14 us: hop(): return lax.ppermute(x, 'left', pairs)]
    unnamed x2 -> x11, local copies, waits for them, and re-layouts: 0.01 us -> 4.8 us
  transfers between devices with their start and end apart: 2 -> 13, of which waited for: 2 -> 4; matrix products, arithmetic and copies ran while one was open for 0% -> 6% of each run, Pallas kernels for 0% -> 9%
where the time goes in v1:
time: 113 us
  waiting for transfers between devices  67.4 us (60%)
  Pallas kernels  19.3 us (17%)
  starting transfers between devices  17 us (15%)
  local copies, waits for them, and re-layouts  7.12 us (6%)
  other arithmetic  1.62 us (1%)
    ppermute x3, waiting for transfers between devices, partner(): return lax.ppermute(x, 'right', [(i, i ^ step) for i in range(4)])  37.8 us
    ppermute x10, waiting for transfers between devices, hop(): return lax.ppermute(x, 'left', pairs)  29.6 us
    pallas_call x2, Pallas kernels, pair_features(): pl.pallas_call(functools.partial(kernel, line, nl, nr, part), out_shape=j...  19.3 us
    ppermute x10, starting transfers between devices, hop(): return lax.ppermute(x, 'left', pairs)  14 us
    unnamed x11, local copies, waits for them, and re-layouts  4.8 us
    ppermute x3, starting transfers between devices, partner(): return lax.ppermute(x, 'right', [(i, i ^ step) for i in range(4)])  2.97 us
  transfers between devices with their start and end apart: 13, of which 4 were waited for; matrix products, arithmetic and copies ran while one was open for 6% of the time, Pallas kernels for 9%

profile of v1, /device:TPU:0, one launch (start us, length us, event | category | flops | bytes accessed | tf_op | source)
XLA Modules:
  0.0 112.8 jit_solution(11072600790590942630)
XLA Ops:
  0.0 3.0 %collective-permute-start.1 = (bf16[512,2048]{1,0:T(8,128)(2,1)}, bf16[512,2048]{1,0:T(8,128)(2,1)S(1)}, u32[]{:S(2)}, u32[]{:S(2)}) collective-permute-start(bf16[512,2048]{1,0:T(8,128)(2,1)} %refs_0_.3), channel_id=1, source_target_pairs={{0,8},{4,12},{8,0},{12,4},{1,9},{5,13},{9,1},{13,5},{2,10},{6,14},... | collective-permute-start | bytes 6291464 | tf_op jit(solution)/shard_map/ppermute | solution.py:159
  3.0 1.3 %fusion = (bf16[512,512]{1,0:T(8,128)(2,1)S(1)}, bf16[512,512]{1,0:T(8,128)(2,1)S(1)}) fusion(bf16[512,1024]{1,0:T(8,128)(2,1)} %param.5), kind=kLoop, calls=%fused_computation.4 | loop fusion | bytes 2097152 | tf_op jit(solution)/shard_map/split | solution.py:161
  4.2 1.6 %collective-permute-start.8 = (bf16[512,512]{1,0:T(8,128)(2,1)S(1)}, bf16[512,512]{1,0:T(8,128)(2,1)S(1)}, u32[]{:S(2)}, u32[]{:S(2)}) collective-permute-start(bf16[512,512]{1,0:T(8,128)(2,1)S(1)} %get-tuple-element.21.refs_4_), channel_id=1, source_target_pairs={{0,1},{1,0},{2,3},{3,2},{4,5},{5,4},{6,7},{7,6},{8,9},{9,8},{10,11... | collective-permute-start | bytes 1572872 | tf_op jit(solution)/shard_map/ppermute | solution.py:156
  5.9 0.7 collective-permute-start.9
  6.6 4.4 %collective-permute-start.3 = (bf16[512,512]{1,0:T(8,128)(2,1)S(1)}, bf16[512,512]{1,0:T(8,128)(2,1)S(1)}, u32[]{:S(2)}, u32[]{:S(2)}) collective-permute-start(bf16[512,512]{1,0:T(8,128)(2,1)S(1)} %get-tuple-element.22.refs_4_), channel_id=1, source_target_pairs={{0,1},{1,0},{2,3},{3,2},{4,5},{5,4},{6,7},{7,6},{8,9},{9,8},{10,11... | collective-permute-start | bytes 1572872 | tf_op jit(solution)/shard_map/ppermute | solution.py:156
  11.0 37.8 %collective-permute-done.1.refs_2_ = bf16[512,2048]{1,0:T(8,128)(2,1)S(1)} collective-permute-done((bf16[512,2048]{1,0:T(8,128)(2,1)}, bf16[512,2048]{1,0:T(8,128)(2,1)S(1)}, u32[]{:S(2)}, u32[]{:S(2)}) %collective-permute-start.1) | collective-permute-done | bytes 2097184 | tf_op jit(solution)/shard_map/ppermute | solution.py:159
  48.8 0.7 collective-permute-start.4
  49.5 1.3 %collective-permute-start.10 = (bf16[512,512]{1,0:T(8,128)(2,1)S(1)}, bf16[512,512]{1,0:T(8,128)(2,1)S(1)}, u32[]{:S(2)}, u32[]{:S(2)}) collective-permute-start(bf16[512,512]{1,0:T(8,128)(2,1)S(1)} %collective-permute-done.9.refs_6_), channel_id=1, source_target_pairs={{1,0},{2,3},{5,4},{6,7},{9,8},{10,11},{13,12},{14,15},{17,16},{18,... | collective-permute-start | bytes 1572872 | tf_op jit(solution)/shard_map/ppermute | solution.py:156
  50.8 0.7 collective-permute-start.11
  51.5 1.1 copy.6
  52.6 1.3 %collective-permute-start.5 = (bf16[512,512]{1,0:T(8,128)(2,1)S(1)}, bf16[512,512]{1,0:T(8,128)(2,1)S(1)}, u32[]{:S(2)}, u32[]{:S(2)}) collective-permute-start(bf16[512,512]{1,0:T(8,128)(2,1)S(1)} %collective-permute-done.4.refs_6_), channel_id=1, source_target_pairs={{1,0},{2,3},{5,4},{6,7},{9,8},{10,11},{13,12},{14,15},{17,16},{18,... | collective-permute-start | bytes 1572872 | tf_op jit(solution)/shard_map/ppermute | solution.py:156
  53.9 13.8 %collective-permute-done.10.refs_7_ = bf16[512,512]{1,0:T(8,128)(2,1)S(1)} collective-permute-done((bf16[512,512]{1,0:T(8,128)(2,1)S(1)}, bf16[512,512]{1,0:T(8,128)(2,1)S(1)}, u32[]{:S(2)}, u32[]{:S(2)}) %collective-permute-start.10) | collective-permute-done | bytes 524320 | tf_op jit(solution)/shard_map/ppermute | solution.py:156
  67.7 0.7 collective-permute-start.6
  68.4 1.3 %collective-permute-start.12 = (bf16[512,512]{1,0:T(8,128)(2,1)S(1)}, bf16[512,512]{1,0:T(8,128)(2,1)S(1)}, u32[]{:S(2)}, u32[]{:S(2)}) collective-permute-start(bf16[512,512]{1,0:T(8,128)(2,1)S(1)} %collective-permute-done.11.refs_8_), channel_id=1, source_target_pairs={{1,0},{2,3},{5,4},{6,7},{9,8},{10,11},{13,12},{14,15},{17,16},{18,... | collective-permute-start | bytes 1572872 | tf_op jit(solution)/shard_map/ppermute | solution.py:156
  69.7 1.6 %broadcast_select_fusion = bf16[32,4,32,4,128]{4,3,2,1,0:T(4,128)(2,1)S(1)} fusion(pred[4,4]{1,0:T(4,128)(4,1)S(1)} %iota_compare_fusion, bf16[32,32,128]{2,1,0:T(8,128)(2,1)S(1)} %copy.6), kind=kLoop, calls=%fused_computation.1 | loop fusion | flops 2097152 | bytes 4456464 | tf_op jit(solution)/shard_map/jit(_where)/select_n | solution.py:21
  71.3 0.0 copy-start.4
  71.3 2.7 %copy.9 = bf16[512,8,4,128]{3,1,2,0:T(8,128)(2,1)} copy(bf16[512,8,4,128]{3,2,1,0:T(4,128)(2,1)S(1)} %bitcast.12) | data formatting | bytes 8388608
  74.0 5.9 %collective-permute-done.5.refs_7_ = bf16[512,512]{1,0:T(8,128)(2,1)S(1)} collective-permute-done((bf16[512,512]{1,0:T(8,128)(2,1)S(1)}, bf16[512,512]{1,0:T(8,128)(2,1)S(1)}, u32[]{:S(2)}, u32[]{:S(2)}) %collective-permute-start.5) | collective-permute-done | bytes 524320 | tf_op jit(solution)/shard_map/ppermute | solution.py:156
  79.9 1.3 %collective-permute-start.7 = (bf16[512,512]{1,0:T(8,128)(2,1)S(1)}, bf16[512,512]{1,0:T(8,128)(2,1)S(1)}, u32[]{:S(2)}, u32[]{:S(2)}) collective-permute-start(bf16[512,512]{1,0:T(8,128)(2,1)S(1)} %collective-permute-done.6.refs_8_), channel_id=1, source_target_pairs={{1,0},{2,3},{5,4},{6,7},{9,8},{10,11},{13,12},{14,15},{17,16},{18,... | collective-permute-start | bytes 1572872 | tf_op jit(solution)/shard_map/ppermute | solution.py:156
  81.2 9.9 %collective-permute-done.12.refs_9_ = bf16[512,512]{1,0:T(8,128)(2,1)S(1)} collective-permute-done((bf16[512,512]{1,0:T(8,128)(2,1)S(1)}, bf16[512,512]{1,0:T(8,128)(2,1)S(1)}, u32[]{:S(2)}, u32[]{:S(2)}) %collective-permute-start.12) | collective-permute-done | bytes 524320 | tf_op jit(solution)/shard_map/ppermute | solution.py:156
  91.2 1.3 %copy-done.2 = bf16[512,2048]{1,0:T(8,128)(2,1)} copy-done((bf16[512,2048]{1,0:T(8,128)(2,1)}, bf16[512,2048]{1,0:T(8,128)(2,1)S(1)}, u32[]{:S(2)}) %copy-start.2) | copy-done | bytes 2097176
  92.5 0.8 copy-done.3
  93.3 9.6 %shard_map.46.refs_12_ = f32[64,32,128]{2,1,0:T(8,128)} custom-call(bf16[512,2048]{1,0:T(8,128)(2,1)S(1)} %copy-done, bf16[512,2048]{1,0:T(8,128)(2,1)} %copy-done.2, bf16[512,2048]{1,0:T(8,128)(2,1)} %copy-done.1, bf16[512,2048]{1,0:T(8,128)(2,1)} %copy-done.3, bf16[512,512]{1,0:T(8,128)(2,1)S(1)} %get-tuple-element.21.refs_4_, ...), custom_call_target="tpu_custom_call" | custom-call | flops 4294967296 | bytes 10485760 | tf_op jit(solution)/shard_map/pallas_call | solution.py:121
  102.9 9.7 %shard_map.47 = f32[64,32,128]{2,1,0:T(8,128)} custom-call(bf16[512,2048]{1,0:T(8,128)(2,1)S(1)} %copy-done, bf16[512,2048]{1,0:T(8,128)(2,1)} %copy-done.2, bf16[512,2048]{1,0:T(8,128)(2,1)} %copy-done.1, bf16[512,2048]{1,0:T(8,128)(2,1)} %copy-done.3, bf16[512,512]{1,0:T(8,128)(2,1)S(1)} %get-tuple-element.22.refs_4_, ...), custom_call_target="tpu_custom_call", output_to_operand_aliasing={{}: (12, {})} | custom-call | flops 4294967296 | bytes 10485760 | tf_op jit(solution)/shard_map/pallas_call | solution.py:121
  (21 shorter events, 0.1 us)
Async XLA Ops:
  0.0 48.8 %collective-permute-start.1 = (bf16[512,2048]{1,0:T(8,128)(2,1)}, bf16[512,2048]{1,0:T(8,128)(2,1)S(1)}, u32[]{:S(2)}, u32[]{:S(2)}) collective-permute-start(bf16[512,2048]{1,0:T(8,128)(2,1)} %refs_0_.3), channel_id=1, source_target_pairs={{0,8},{4,12},{8,0},{12,4},{1,9},{5,13},{9,1},{13,5},{2,10},{6,14},... | collective-permute-start | bytes 6291464 | tf_op jit(solution)/shard_map/ppermute | solution.py:159
  4.2 44.6 %collective-permute-start.8 = (bf16[512,512]{1,0:T(8,128)(2,1)S(1)}, bf16[512,512]{1,0:T(8,128)(2,1)S(1)}, u32[]{:S(2)}, u32[]{:S(2)}) collective-permute-start(bf16[512,512]{1,0:T(8,128)(2,1)S(1)} %get-tuple-element.21.refs_4_), channel_id=1, source_target_pairs={{0,1},{1,0},{2,3},{3,2},{4,5},{5,4},{6,7},{7,6},{8,9},{9,8},{10,11... | collective-permute-start | bytes 1572872 | tf_op jit(solution)/shard_map/ppermute | solution.py:156
  5.9 43.6 %collective-permute-start.9 = (bf16[512,512]{1,0:T(8,128)(2,1)S(1)}, bf16[512,512]{1,0:T(8,128)(2,1)S(1)}, u32[]{:S(2)}, u32[]{:S(2)}) collective-permute-start(bf16[512,512]{1,0:T(8,128)(2,1)S(1)} %get-tuple-element.21.refs_4_), channel_id=1, source_target_pairs={{1,2},{2,1},{5,6},{6,5},{9,10},{10,9},{13,14},{14,13},{17,18},{18,... | collective-permute-start | bytes 1572872 | tf_op jit(solution)/shard_map/ppermute | solution.py:156
  6.6 44.3 %collective-permute-start.3 = (bf16[512,512]{1,0:T(8,128)(2,1)S(1)}, bf16[512,512]{1,0:T(8,128)(2,1)S(1)}, u32[]{:S(2)}, u32[]{:S(2)}) collective-permute-start(bf16[512,512]{1,0:T(8,128)(2,1)S(1)} %get-tuple-element.22.refs_4_), channel_id=1, source_target_pairs={{0,1},{1,0},{2,3},{3,2},{4,5},{5,4},{6,7},{7,6},{8,9},{9,8},{10,11... | collective-permute-start | bytes 1572872 | tf_op jit(solution)/shard_map/ppermute | solution.py:156
  11.0 80.1 %collective-permute-start = (bf16[512,2048]{1,0:T(8,128)(2,1)}, bf16[512,2048]{1,0:T(8,128)(2,1)S(1)}, u32[]{:S(2)}, u32[]{:S(2)}) collective-permute-start(bf16[512,2048]{1,0:T(8,128)(2,1)} %refs_0_.3), channel_id=1, source_target_pairs={{0,4},{4,0},{8,12},{12,8},{1,5},{5,1},{9,13},{13,9},{2,6},{6,2},{1... | collective-permute-start | bytes 6291464 | tf_op jit(solution)/shard_map/ppermute | solution.py:159
  48.8 25.2 %copy-start.1 = (bf16[512,2048]{1,0:T(8,128)(2,1)}, bf16[512,2048]{1,0:T(8,128)(2,1)S(1)}, u32[]{:S(2)}) copy-start(bf16[512,2048]{1,0:T(8,128)(2,1)S(1)} %collective-permute-done.1.refs_2_) | copy-start | bytes 6291460
  48.8 42.3 %collective-permute-start.2 = (bf16[512,2048]{1,0:T(8,128)(2,1)S(1)}, bf16[512,2048]{1,0:T(8,128)(2,1)S(1)}, u32[]{:S(2)}, u32[]{:S(2)}) collective-permute-start(bf16[512,2048]{1,0:T(8,128)(2,1)S(1)} %collective-permute-done.1.refs_2_), channel_id=1, source_target_pairs={{0,4},{4,0},{8,12},{12,8},{1,5},{5,1},{9,13},{13,9},{2,6},{6,2},{1... | collective-permute-start | bytes 6291464 | tf_op jit(solution)/shard_map/ppermute | solution.py:159
  48.8 3.8 %collective-permute-start.4 = (bf16[512,512]{1,0:T(8,128)(2,1)S(1)}, bf16[512,512]{1,0:T(8,128)(2,1)S(1)}, u32[]{:S(2)}, u32[]{:S(2)}) collective-permute-start(bf16[512,512]{1,0:T(8,128)(2,1)S(1)} %get-tuple-element.22.refs_4_), channel_id=1, source_target_pairs={{1,2},{2,1},{5,6},{6,5},{9,10},{10,9},{13,14},{14,13},{17,18},{18,... | collective-permute-start | bytes 1572872 | tf_op jit(solution)/shard_map/ppermute | solution.py:156
  49.5 18.2 %collective-permute-start.10 = (bf16[512,512]{1,0:T(8,128)(2,1)S(1)}, bf16[512,512]{1,0:T(8,128)(2,1)S(1)}, u32[]{:S(2)}, u32[]{:S(2)}) collective-permute-start(bf16[512,512]{1,0:T(8,128)(2,1)S(1)} %collective-permute-done.9.refs_6_), channel_id=1, source_target_pairs={{1,0},{2,3},{5,4},{6,7},{9,8},{10,11},{13,12},{14,15},{17,16},{18,... | collective-permute-start | bytes 1572872 | tf_op jit(solution)/shard_map/ppermute | solution.py:156
  50.8 17.6 %collective-permute-start.11 = (bf16[512,512]{1,0:T(8,128)(2,1)S(1)}, bf16[512,512]{1,0:T(8,128)(2,1)S(1)}, u32[]{:S(2)}, u32[]{:S(2)}) collective-permute-start(bf16[512,512]{1,0:T(8,128)(2,1)S(1)} %collective-permute-done.8.refs_5_), channel_id=1, source_target_pairs={{1,2},{2,1},{5,6},{6,5},{9,10},{10,9},{13,14},{14,13},{17,18},{18,... | collective-permute-start | bytes 1572872 | tf_op jit(solution)/shard_map/ppermute | solution.py:156
  52.6 27.3 %collective-permute-start.5 = (bf16[512,512]{1,0:T(8,128)(2,1)S(1)}, bf16[512,512]{1,0:T(8,128)(2,1)S(1)}, u32[]{:S(2)}, u32[]{:S(2)}) collective-permute-start(bf16[512,512]{1,0:T(8,128)(2,1)S(1)} %collective-permute-done.4.refs_6_), channel_id=1, source_target_pairs={{1,0},{2,3},{5,4},{6,7},{9,8},{10,11},{13,12},{14,15},{17,16},{18,... | collective-permute-start | bytes 1572872 | tf_op jit(solution)/shard_map/ppermute | solution.py:156
  67.7 12.2 %collective-permute-start.6 = (bf16[512,512]{1,0:T(8,128)(2,1)S(1)}, bf16[512,512]{1,0:T(8,128)(2,1)S(1)}, u32[]{:S(2)}, u32[]{:S(2)}) collective-permute-start(bf16[512,512]{1,0:T(8,128)(2,1)S(1)} %collective-permute-done.3.refs_5_), channel_id=1, source_target_pairs={{1,2},{2,1},{5,6},{6,5},{9,10},{10,9},{13,14},{14,13},{17,18},{18,... | collective-permute-start | bytes 1572872 | tf_op jit(solution)/shard_map/ppermute | solution.py:156
  68.4 22.7 %collective-permute-start.12 = (bf16[512,512]{1,0:T(8,128)(2,1)S(1)}, bf16[512,512]{1,0:T(8,128)(2,1)S(1)}, u32[]{:S(2)}, u32[]{:S(2)}) collective-permute-start(bf16[512,512]{1,0:T(8,128)(2,1)S(1)} %collective-permute-done.11.refs_8_), channel_id=1, source_target_pairs={{1,0},{2,3},{5,4},{6,7},{9,8},{10,11},{13,12},{14,15},{17,16},{18,... | collective-permute-start | bytes 1572872 | tf_op jit(solution)/shard_map/ppermute | solution.py:156
  71.3 2.7 %copy-start.4 = (s32[64,32]{0,1:T(8,128)S(1)}, s32[64,32]{0,1:T(8,128)}, u32[]{:S(2)}) copy-start(s32[64,32]{0,1:T(8,128)} %param.6) | copy-start | bytes 24580
  71.3 21.9 %copy-start = (bf16[512,2048]{1,0:T(8,128)(2,1)S(1)}, bf16[512,2048]{1,0:T(8,128)(2,1)}, u32[]{:S(2)}) copy-start(bf16[512,2048]{1,0:T(8,128)(2,1)} %refs_0_.3) | copy-start | bytes 6291460
  79.9 23.0 %collective-permute-start.7 = (bf16[512,512]{1,0:T(8,128)(2,1)S(1)}, bf16[512,512]{1,0:T(8,128)(2,1)S(1)}, u32[]{:S(2)}, u32[]{:S(2)}) collective-permute-start(bf16[512,512]{1,0:T(8,128)(2,1)S(1)} %collective-permute-done.6.refs_8_), channel_id=1, source_target_pairs={{1,0},{2,3},{5,4},{6,7},{9,8},{10,11},{13,12},{14,15},{17,16},{18,... | collective-permute-start | bytes 1572872 | tf_op jit(solution)/shard_map/ppermute | solution.py:156
  91.1 1.4 %copy-start.2 = (bf16[512,2048]{1,0:T(8,128)(2,1)}, bf16[512,2048]{1,0:T(8,128)(2,1)S(1)}, u32[]{:S(2)}) copy-start(bf16[512,2048]{1,0:T(8,128)(2,1)S(1)} %collective-permute-done.refs_1_) | copy-start | bytes 6291460
  91.1 2.1 %copy-start.3 = (bf16[512,2048]{1,0:T(8,128)(2,1)}, bf16[512,2048]{1,0:T(8,128)(2,1)S(1)}, u32[]{:S(2)}) copy-start(bf16[512,2048]{1,0:T(8,128)(2,1)S(1)} %collective-permute-done.2.refs_3_) | copy-start | bytes 6291460

commit v2 on v0

v2 whole, which is shorter than its diff:
```python
import functools

import jax
import jax.numpy as jnp
from jax import lax
from jax.experimental import pallas as pl
from jax.experimental.pallas import tpu as pltpu
from jax.sharding import PartitionSpec as P

CH = 32
LANES = 128
GROUP = LANES // CH
CORES = 2
FIRST_PART, PART_UNITS = 1, 2
LEFT_PARTS = 4
EARLY_VMEM = 40 * 2**20
LATE_VMEM = 24 * 2**20


def spread_weights(w_out):
    pair = w_out.shape[1]
    by_e = w_out.reshape(CH, CH, pair).transpose(1, 0, 2)
    same = jnp.eye(GROUP, dtype=jnp.bool_)[None, :, None, :, None]
    full = jnp.where(same, by_e[:, None, :, None, :], jnp.zeros((), w_out.dtype))
    return full.reshape(CH * LANES, GROUP * pair)


def turned(right, perm):
    return lax.dot_general(perm, right, (((1,), (1,)), ((), ())), preferred_element_type=jnp.float32).astype(
        jnp.bfloat16
    )


def regroup(cols):
    res = cols // CH
    to = lax.broadcasted_iota(jnp.int32, (cols, cols), 0)
    source = lax.broadcasted_iota(jnp.int32, (cols, cols), 1)
    return jnp.where(source == (to % res) * CH + to // res, 1.0, 0.0).astype(jnp.bfloat16)


def early_kernel(places, *refs):
    nl = len(places)
    parts = (len(refs) - nl - 4) // 5
    lefts = refs[:nl]
    rights = refs[nl : nl + 4 * parts]
    sums = refs[nl + 4 * parts : nl + 5 * parts]
    late_ref, left_v, rt, sem = refs[nl + 5 * parts :]
    l, r = lax.axis_index("left"), lax.axis_index("right")
    end = jnp.logical_or(l == 0, l == 3)
    rows = left_v.shape[0] // 3
    flip = 1 - 2 * (r % 2)
    far = (r + 2) % 4
    owners = (r, r + flip, far, far + flip)

    copies = []
    for n, (k, col) in enumerate(places):
        s = owners[k]
        slot = jnp.where(s // 2 == l // 2, (s + l) % 2, jnp.where(l < 2, s, 3 - s))
        at = pl.multiple_of(jnp.minimum(slot, 2) * rows, rows)
        cols = pl.ds(col, lefts[n].shape[1])

        @pl.when(slot < 3)
        def _():
            pltpu.make_async_copy(lefts[n], left_v.at[pl.ds(at, rows), cols], sem.at[n]).start()

        @pl.when(slot == 3)
        def _():
            pltpu.make_async_copy(lefts[n], late_ref.at[:, cols], sem.at[n]).start()

        copies.append(pltpu.make_async_copy(lefts[n], late_ref.at[:, cols], sem.at[n]))

    first_row = 0
    for p in range(parts):
        own, first, mid, outer_end = rights[4 * p : 4 * p + 4]
        cols = own.shape[1]
        perm = regroup(cols)
        here = pl.ds(first_row, cols)
        rt[here, :rows] = turned(own[...], perm)
        rt[here, rows : 2 * rows] = turned(first[...], perm)

        @pl.when(end)
        def _():
            rt[here, 2 * rows :] = turned(outer_end[...], perm)

        @pl.when(jnp.logical_not(end))
        def _():
            rt[here, 2 * rows :] = turned(mid[...], perm)

        first_row += cols
    for copy in copies:
        copy.wait()
    first_row = 0
    for p in range(parts):
        cols = sums[p].shape[0]
        sums[p][...] = jnp.dot(rt[first_row : first_row + cols, :], left_v[...], preferred_element_type=jnp.float32)
        first_row += cols


def early_sums(places, lefts, rights):
    rows, width = lefts[0].shape
    vmem = pl.BlockSpec(memory_space=pltpu.VMEM)
    anywhere = pl.BlockSpec(memory_space=pl.ANY)
    parts = len(rights)
    cols = [part[0].shape[1] for part in rights]
    out = pl.pallas_call(
        functools.partial(early_kernel, places),
        out_shape=[jax.ShapeDtypeStruct((c, width), jnp.float32) for c in cols]
        + [jax.ShapeDtypeStruct((rows, width), jnp.bfloat16)],
        in_specs=[anywhere] * len(lefts) + [vmem] * (4 * parts),
        out_specs=[vmem] * parts + [anywhere],
        scratch_shapes=[
            pltpu.VMEM((3 * rows, width), jnp.bfloat16),
            pltpu.VMEM((sum(cols), 3 * rows), jnp.bfloat16),
            pltpu.SemaphoreType.DMA((len(lefts),)),
        ],
        compiler_params=pltpu.CompilerParams(vmem_limit_bytes=EARLY_VMEM),
        cost_estimate=pl.CostEstimate(flops=1, bytes_accessed=1, transcendentals=0),
    )(*lefts, *[x for part in rights for x in part])
    return out[:parts], out[parts]


def late_kernel(line, start, *refs):
    if line:
        sums, left, mid, outer_end, wide, counts = refs[:6]
    else:
        left, mid, wide, counts = refs[:4]
    out_ref, rt, lhs, out_v, sem = refs[-5:]
    cols, rows = rt.shape
    width = left.shape[1]
    res = cols // CH
    perm = regroup(cols)
    if line:
        l = lax.axis_index("left")
        end = jnp.logical_or(l == 0, l == 3)

        @pl.when(end)
        def _():
            rt[...] = turned(outer_end[...], perm)

        @pl.when(jnp.logical_not(end))
        def _():
            rt[...] = turned(mid[...], perm)

    else:
        rt[...] = turned(mid[...], perm)
    total = jnp.dot(rt[...], left[...], preferred_element_type=jnp.float32)
    if line:
        total += sums[...]
    outer = total.astype(jnp.bfloat16)
    for g in range(width // LANES):
        for e in range(CH):
            lhs[g * res : (g + 1) * res, e * LANES : (e + 1) * LANES] = outer[
                e * res : (e + 1) * res, g * LANES : (g + 1) * LANES
            ]
    projected = jnp.dot(lhs[...], wide[...], preferred_element_type=jnp.float32)
    pair = out_v.shape[2]
    for g in range(width // LANES):
        for i in range(GROUP):
            row = g * GROUP + i
            out_v[row] = projected[g * res : (g + 1) * res, i * pair : (i + 1) * pair] / counts[:, row : row + 1]
    out_copy = pltpu.make_async_copy(out_v, out_ref.at[:, pl.ds(start, res), :], sem)
    out_copy.start()
    out_copy.wait()


def pair_features(line, start, operands, counts, right_dev, before):
    vmem = pl.BlockSpec(memory_space=pltpu.VMEM)
    anywhere = pl.BlockSpec(memory_space=pl.ANY)
    left, right, wide = (operands[1], operands[2], operands[4]) if line else operands
    rows, width = left.shape
    cols = right.shape[1]
    res, left_dev = cols // CH, width // CH
    pair = wide.shape[1] // GROUP
    operands = [*operands, counts]
    specs = [vmem] * len(operands)
    aliases = {}
    if before is not None:
        aliases = {len(operands): 0}
        operands.append(before)
        specs.append(anywhere)
    return pl.pallas_call(
        functools.partial(late_kernel, line, start),
        out_shape=jax.ShapeDtypeStruct((left_dev, right_dev, pair), jnp.float32),
        in_specs=specs,
        out_specs=anywhere,
        input_output_aliases=aliases,
        scratch_shapes=[
            pltpu.VMEM((cols, rows), jnp.bfloat16),
            pltpu.VMEM((width // LANES * res, CH * LANES), jnp.bfloat16),
            pltpu.VMEM((left_dev, res, pair), jnp.float32),
            pltpu.SemaphoreType.DMA,
        ],
        compiler_params=pltpu.CompilerParams(vmem_limit_bytes=LATE_VMEM if line else 2 * LATE_VMEM),
        cost_estimate=pl.CostEstimate(flops=1, bytes_accessed=1, transcendentals=0),
    )(*operands)


def tied(*values):
    return lax.optimization_barrier(values)


def gather_line(left_act, right_act):
    ends = ((0, 1), (1, 0), (2, 3), (3, 2))
    middle = ((1, 2), (2, 1))
    outward = ((1, 0), (2, 3))

    def hop(x, pairs):
        return lax.ppermute(x, "left", pairs)

    def partner(x, step):
        return lax.ppermute(x, "right", [(i, i ^ step) for i in range(4)])

    cut = right_act.shape[1] * FIRST_PART // PART_UNITS
    a, c = right_act[:, :cut], right_act[:, cut:]
    width = left_act.shape[1] // LEFT_PARTS
    quarters = [left_act[:, n * width : (n + 1) * width] for n in range(LEFT_PARTS)]
    near = partner(left_act, 1)
    a1, a2, far0 = hop(a, ends), hop(a, middle), partner(quarters[0], CORES)
    c1, c2, far1 = hop(c, ends), hop(c, middle), partner(quarters[1], CORES)
    a1, a2, far0, quarters[2] = tied(a1, a2, far0, quarters[2])
    a3, a4, far2 = hop(a2, outward), hop(a1, middle), partner(quarters[2], CORES)
    c1, c2, far1, quarters[3] = tied(c1, c2, far1, quarters[3])
    c3, c4, far3 = hop(c2, outward), hop(c1, middle), partner(quarters[3], CORES)
    a3, a4, far2 = tied(a3, a4, far2)
    a5 = hop(a4, outward)
    cross = [partner(x, 1) for x in (far0, far2)]
    c3, c4, far3 = tied(c3, c4, far3)
    c5 = hop(c4, outward)
    cross += [partner(x, 1) for x in (far1, far3)]
    lefts = [left_act, near, far0, far2, far1, far3, *cross]
    order = [0, 2, 1, 3]
    places = [(0, 0), (1, 0)] + [(2, n * width) for n in order] + [(3, n * width) for n in order]
    return places, lefts, ((a, a1, a2, a3), (c, c1, c2, c3)), ((a4, a5), (c4, c5))


def shards(line, left_act, right_act, counts, w_out):
    right_dev = counts.shape[1]
    cut = right_dev * FIRST_PART // PART_UNITS
    by_right = counts.astype(jnp.float32).T
    count_parts = (by_right[:cut], by_right[cut:])
    wide = spread_weights(w_out)
    if line:
        places, lefts, early, late = gather_line(left_act, right_act)
        sums, left_late = early_sums(places, lefts, early)
        operands = [(sums[p], left_late, *late[p], wide) for p in range(2)]
    else:
        left_full = lax.all_gather(left_act, "right", axis=0, tiled=True)
        full = lax.all_gather(right_act, "left", axis=0, tiled=True)
        operands = [(left_full, x, wide) for x in (full[:, : cut * CH], full[:, cut * CH :])]
    out = None
    for start, given, count in zip((0, cut), operands, count_parts):
        out = pair_features(line, start, given, count, right_dev, out)
    return out


def solution(mesh):
    in_specs = (
        P(("groups", "right"), "left"),
        P(("groups", "left"), "right"),
        P(("groups", "left"), "right"),
        P(),
    )
    out_specs = P(("groups", "left"), "right", None)
    line = mesh.shape["left"] == 4 and mesh.shape["right"] == 4
    body = functools.partial(shards, line)
    return jax.shard_map(body, mesh=mesh, in_specs=in_specs, out_specs=out_specs, check_vma=False)
```

time: 222 us -> 86.7 us (0.39)
  waiting for transfers between devices: 143 us -> 38.2 us
  local copies, waits for them, and re-layouts: 42.1 us -> 6.29 us
  starting transfers between devices: 0.04 us -> 20 us
  matrix products: 19.7 us -> 0 us
  Pallas kernels: 0 us -> 19.7 us
  between operations: 13.4 us -> 0.42 us
    all_gather x2 -> x0, waiting for transfers between devices: 142 us -> none  [the longest x1 83.6 us: shards(): lax.all_gather(right_act, 'left', axis=0, tiled=True)]
    convert_element_type x3 -> x0, local copies, waits for them, and re-layouts: 42.1 us -> none  [the longest x2 42 us: shards(): flat = flat.astype(jnp.bfloat16)]
    ppermute x0 -> x19, waiting for transfers between devices: none -> 38.2 us  [the longest x10 25.4 us: hop(): return lax.ppermute(x, 'left', pairs)]
    ppermute x0 -> x19, starting transfers between devices: none -> 20 us  [the longest x10 13.9 us: hop(): return lax.ppermute(x, 'left', pairs)]
    pallas_call x0 -> x3, Pallas kernels: none -> 19.7 us  [the longest x1 12 us: early_sums(): pl.pallas_call(functools.partial(early_kernel, places), out_shape=[jax.Sh...]
    dot_general x2 -> x0, matrix products: 19.7 us -> none  [the longest x1 14 us: contract_rows(): lax.dot_general(first, second, (((0,), (0,)), ((), ())), preferred_elemen...]
    unnamed x2 -> x15, local copies, waits for them, and re-layouts: 0.01 us -> 4.29 us
  transfers between devices with their start and end apart: 2 -> 19, of which waited for: 2 -> 8; matrix products, arithmetic and copies ran while one was open for 0% -> 3% of each run, Pallas kernels for 0% -> 18%
where the time goes in v2:
time: 86.7 us; the launch traced here: 86.3 us
  waiting for transfers between devices  38.2 us (44%)
  starting transfers between devices  20 us (23%)
  Pallas kernels  19.7 us (23%)
  local copies, waits for them, and re-layouts  6.29 us (7%)
  other arithmetic  1.62 us (2%)
    ppermute x10, waiting for transfers between devices, hop(): return lax.ppermute(x, 'left', pairs)  25.4 us
    ppermute x10, starting transfers between devices, hop(): return lax.ppermute(x, 'left', pairs)  13.9 us
    ppermute x9, waiting for transfers between devices, partner(): return lax.ppermute(x, 'right', [(i, i ^ step) for i in range(4)])  12.9 us
    pallas_call x1, Pallas kernels, early_sums(): pl.pallas_call(functools.partial(early_kernel, places), out_shape=[jax.Sh...  12 us
    pallas_call x2, Pallas kernels, pair_features(): pl.pallas_call(functools.partial(late_kernel, line, start), out_shape=jax...  7.72 us
    ppermute x9, starting transfers between devices, partner(): return lax.ppermute(x, 'right', [(i, i ^ step) for i in range(4)])  6.16 us
    unnamed x15, local copies, waits for them, and re-layouts  4.29 us
    slice x1, local copies, waits for them, and re-layouts, gather_line(): left_act[:, n * width:(n + 1) * width]  1.82 us
  transfers between devices with their start and end apart: 19, of which 8 were waited for; matrix products, arithmetic and copies ran while one was open for 3% of the time, Pallas kernels for 18%

profile of v2, /device:TPU:0, one launch (start us, length us, event | category | flops | bytes accessed | tf_op | source)
XLA Modules:
  0.0 86.3 jit_solution(14324698426911546174)
XLA Ops:
  0.0 1.8 %fusion = (bf16[512,512]{1,0:T(8,128)(2,1)S(1)}, bf16[512,512]{1,0:T(8,128)(2,1)S(1)}, bf16[512,512]{1,0:T(8,128)(2,1)S(1)}, bf16[512,512]{1,0:T(8,128)(2,1)S(1)}) fusion(bf16[512,2048]{1,0:T(8,128)(2,1)} %refs_0_.1), kind=kLoop, calls=%fused_computation.4 | loop fusion | bytes 4194304 | tf_op jit(solution)/shard_map/slice | solution.py:216
  1.8 3.0 %collective-permute-start.9 = (bf16[512,512]{1,0:T(8,128)(2,1)S(1)}, bf16[512,512]{1,0:T(8,128)(2,1)S(1)}, u32[]{:S(2)}, u32[]{:S(2)}) collective-permute-start(bf16[512,512]{1,0:T(8,128)(2,1)S(1)} %get-tuple-element.40), channel_id=1, source_target_pairs={{0,8},{4,12},{8,0},{12,4},{1,9},{5,13},{9,1},{13,5},{2,10},{6,14},... | collective-permute-start | bytes 1572872 | tf_op jit(solution)/shard_map/ppermute | solution.py:211
  5.0 1.6 %collective-permute-start.7 = (bf16[512,512]{1,0:T(8,128)(2,1)S(1)}, bf16[512,512]{1,0:T(8,128)(2,1)S(1)}, u32[]{:S(2)}, u32[]{:S(2)}) collective-permute-start(bf16[512,512]{1,0:T(8,128)(2,1)S(1)} %get-tuple-element.43.refs_14_), channel_id=1, source_target_pairs={{0,1},{1,0},{2,3},{3,2},{4,5},{5,4},{6,7},{7,6},{8,9},{9,8},{10,11... | collective-permute-start | bytes 1572872 | tf_op jit(solution)/shard_map/ppermute | solution.py:208
  7.9 4.4 %collective-permute-start.1 = (bf16[512,512]{1,0:T(8,128)(2,1)S(1)}, bf16[512,512]{1,0:T(8,128)(2,1)S(1)}, u32[]{:S(2)}, u32[]{:S(2)}) collective-permute-start(bf16[512,512]{1,0:T(8,128)(2,1)S(1)} %get-tuple-element.44.refs_10_), channel_id=1, source_target_pairs={{0,1},{1,0},{2,3},{3,2},{4,5},{5,4},{6,7},{7,6},{8,9},{9,8},{10,11... | collective-permute-start | bytes 1572872 | tf_op jit(solution)/shard_map/ppermute | solution.py:208
  12.2 5.4 %collective-permute-done.9.refs_4_ = bf16[512,512]{1,0:T(8,128)(2,1)S(1)} collective-permute-done((bf16[512,512]{1,0:T(8,128)(2,1)S(1)}, bf16[512,512]{1,0:T(8,128)(2,1)S(1)}, u32[]{:S(2)}, u32[]{:S(2)}) %collective-permute-start.9) | collective-permute-done | bytes 524320 | tf_op jit(solution)/shard_map/ppermute | solution.py:211
  18.3 1.6 %collective-permute-done.7.refs_15_ = bf16[512,512]{1,0:T(8,128)(2,1)S(1)} collective-permute-done((bf16[512,512]{1,0:T(8,128)(2,1)S(1)}, bf16[512,512]{1,0:T(8,128)(2,1)S(1)}, u32[]{:S(2)}, u32[]{:S(2)}) %collective-permute-start.7) | collective-permute-done | bytes 524320 | tf_op jit(solution)/shard_map/ppermute | solution.py:208
  19.9 1.3 %collective-permute-start.10 = (bf16[512,512]{1,0:T(8,128)(2,1)S(1)}, bf16[512,512]{1,0:T(8,128)(2,1)S(1)}, u32[]{:S(2)}, u32[]{:S(2)}) collective-permute-start(bf16[512,512]{1,0:T(8,128)(2,1)S(1)} %collective-permute-done.8.refs_16_), channel_id=1, source_target_pairs={{1,0},{2,3},{5,4},{6,7},{9,8},{10,11},{13,12},{14,15},{17,16},{18,... | collective-permute-start | bytes 1572872 | tf_op jit(solution)/shard_map/ppermute | solution.py:208
  21.9 6.2 %collective-permute-done.3.refs_2_ = bf16[512,512]{1,0:T(8,128)(2,1)S(1)} collective-permute-done((bf16[512,512]{1,0:T(8,128)(2,1)S(1)}, bf16[512,512]{1,0:T(8,128)(2,1)S(1)}, u32[]{:S(2)}, u32[]{:S(2)}) %collective-permute-start.3) | collective-permute-done | bytes 524320 | tf_op jit(solution)/shard_map/ppermute | solution.py:211
  28.0 1.7 %collective-permute-start.12 = (bf16[512,512]{1,0:T(8,128)(2,1)S(1)}, bf16[512,512]{1,0:T(8,128)(2,1)S(1)}, u32[]{:S(2)}, u32[]{:S(2)}) collective-permute-start(bf16[512,512]{1,0:T(8,128)(2,1)S(1)} %get-tuple-element.30), channel_id=1, source_target_pairs={{0,8},{4,12},{8,0},{12,4},{1,9},{5,13},{9,1},{13,5},{2,10},{6,14},... | collective-permute-start | bytes 1572872 | tf_op jit(solution)/shard_map/ppermute | solution.py:211
  29.8 1.3 %collective-permute-done.1.refs_11_ = bf16[512,512]{1,0:T(8,128)(2,1)S(1)} collective-permute-done((bf16[512,512]{1,0:T(8,128)(2,1)S(1)}, bf16[512,512]{1,0:T(8,128)(2,1)S(1)}, u32[]{:S(2)}, u32[]{:S(2)}) %collective-permute-start.1) | collective-permute-done | bytes 524320 | tf_op jit(solution)/shard_map/ppermute | solution.py:208
  31.1 1.3 %collective-permute-start.4 = (bf16[512,512]{1,0:T(8,128)(2,1)S(1)}, bf16[512,512]{1,0:T(8,128)(2,1)S(1)}, u32[]{:S(2)}, u32[]{:S(2)}) collective-permute-start(bf16[512,512]{1,0:T(8,128)(2,1)S(1)} %collective-permute-done.2.refs_12_), channel_id=1, source_target_pairs={{1,0},{2,3},{5,4},{6,7},{9,8},{10,11},{13,12},{14,15},{17,16},{18,... | collective-permute-start | bytes 1572872 | tf_op jit(solution)/shard_map/ppermute | solution.py:208
  32.5 9.9 %collective-permute-done.10.refs_17_ = bf16[512,512]{1,0:T(8,128)(2,1)S(1)} collective-permute-done((bf16[512,512]{1,0:T(8,128)(2,1)S(1)}, bf16[512,512]{1,0:T(8,128)(2,1)S(1)}, u32[]{:S(2)}, u32[]{:S(2)}) %collective-permute-start.10) | collective-permute-done | bytes 524320 | tf_op jit(solution)/shard_map/ppermute | solution.py:208
  43.2 8.9 %collective-permute-done.4.refs_13_ = bf16[512,512]{1,0:T(8,128)(2,1)S(1)} collective-permute-done((bf16[512,512]{1,0:T(8,128)(2,1)S(1)}, bf16[512,512]{1,0:T(8,128)(2,1)S(1)}, u32[]{:S(2)}, u32[]{:S(2)}) %collective-permute-start.4) | collective-permute-done | bytes 524320 | tf_op jit(solution)/shard_map/ppermute | solution.py:208
  52.8 1.3 %collective-permute-done.6.refs_3_ = bf16[512,512]{1,0:T(8,128)(2,1)S(1)} collective-permute-done((bf16[512,512]{1,0:T(8,128)(2,1)S(1)}, bf16[512,512]{1,0:T(8,128)(2,1)S(1)}, u32[]{:S(2)}, u32[]{:S(2)}) %collective-permute-start.6) | collective-permute-done | bytes 524320 | tf_op jit(solution)/shard_map/ppermute | solution.py:211
  54.1 1.3 %collective-permute-start.18 = (bf16[512,512]{1,0:T(8,128)(2,1)S(1)}, bf16[512,512]{1,0:T(8,128)(2,1)S(1)}, u32[]{:S(2)}, u32[]{:S(2)}) collective-permute-start(bf16[512,512]{1,0:T(8,128)(2,1)S(1)} %collective-permute-done.5.refs_2_), channel_id=1, source_target_pairs={{1,0},{2,3},{5,4},{6,7},{9,8},{10,11},{13,12},{14,15},{17,16},{18,... | collective-permute-start | bytes 1572872 | tf_op jit(solution)/shard_map/ppermute | solution.py:208
  55.4 1.3 %collective-permute-start.17 = (bf16[512,512]{1,0:T(8,128)(2,1)S(1)}, bf16[512,512]{1,0:T(8,128)(2,1)S(1)}, u32[]{:S(2)}, u32[]{:S(2)}) collective-permute-start(bf16[512,512]{1,0:T(8,128)(2,1)S(1)} %collective-permute-done.11.refs_2_), channel_id=1, source_target_pairs={{1,0},{2,3},{5,4},{6,7},{9,8},{10,11},{13,12},{14,15},{17,16},{18,... | collective-permute-start | bytes 1572872 | tf_op jit(solution)/shard_map/ppermute | solution.py:208
  56.7 1.6 %broadcast_select_fusion = bf16[32,4,32,4,128]{4,3,2,1,0:T(4,128)(2,1)S(1)} fusion(pred[4,4]{1,0:T(4,128)(4,1)S(1)} %iota_compare_fusion, bf16[32,32,128]{2,1,0:T(8,128)(2,1)S(1)} %copy.6), kind=kLoop, calls=%fused_computation.1 | loop fusion | flops 2097152 | bytes 4456464 | tf_op jit(solution)/shard_map/jit(_where)/select_n | solution.py:24
  58.4 0.7 copy.9
  59.2 1.4 %copy-done.3 = bf16[512,2048]{1,0:T(8,128)(2,1)} copy-done((bf16[512,2048]{1,0:T(8,128)(2,1)}, bf16[512,2048]{1,0:T(8,128)(2,1)S(1)}, u32[]{:S(2)}) %copy-start.3) | copy-done | bytes 2097176
  60.5 12.0 %shard_map.46 = (f32[512,2048]{1,0:T(8,128)}, f32[512,2048]{1,0:T(8,128)}, bf16[512,2048]{1,0:T(8,128)(2,1)S(1)}) custom-call(bf16[512,2048]{1,0:T(8,128)(2,1)S(1)} %copy-done, bf16[512,2048]{1,0:T(8,128)(2,1)} %copy-done.3, bf16[512,512]{1,0:T(8,128)(2,1)S(1)} %collective-permute-done.3.refs_2_, bf16[512,512]{1,0:T(8,128)(2,1)S(1)} %collective-permute-done.6.refs_3_, ...), custom_call_target="tpu_custom_call" | custom-call | flops 1 | bytes 1 | tf_op jit(solution)/shard_map/pallas_call | solution.py:105
  72.6 2.2 %copy-done.2 = f32[512,2048]{1,0:T(8,128)S(1)} copy-done((f32[512,2048]{1,0:T(8,128)S(1)}, f32[512,2048]{1,0:T(8,128)}, u32[]{:S(2)}) %copy-start.2) | copy-done | bytes 4194328
  74.7 3.9 %shard_map.47.refs_6_ = f32[64,32,128]{2,1,0:T(8,128)} custom-call(f32[512,2048]{1,0:T(8,128)S(1)} %copy-done.2, bf16[512,2048]{1,0:T(8,128)(2,1)S(1)} %get-tuple-element.35.refs_1_, bf16[512,512]{1,0:T(8,128)(2,1)S(1)} %collective-permute-done.5.refs_2_, bf16[512,512]{1,0:T(8,128)(2,1)S(1)} %collective-permute-done.18.refs_3_, ...), custom_call_target="tpu_custom_call" | custom-call | flops 1 | bytes 1 | tf_op jit(solution)/shard_map/pallas_call | solution.py:181
  78.7 3.7 %collective-permute-done.17.refs_3_ = bf16[512,512]{1,0:T(8,128)(2,1)S(1)} collective-permute-done((bf16[512,512]{1,0:T(8,128)(2,1)S(1)}, bf16[512,512]{1,0:T(8,128)(2,1)S(1)}, u32[]{:S(2)}, u32[]{:S(2)}) %collective-permute-start.17) | collective-permute-done | bytes 524320 | tf_op jit(solution)/shard_map/ppermute | solution.py:208
  82.4 3.8 %shard_map.48 = f32[64,32,128]{2,1,0:T(8,128)} custom-call(f32[512,2048]{1,0:T(8,128)S(1)} %copy-done.1, bf16[512,2048]{1,0:T(8,128)(2,1)S(1)} %get-tuple-element.35.refs_1_, bf16[512,512]{1,0:T(8,128)(2,1)S(1)} %collective-permute-done.11.refs_2_, bf16[512,512]{1,0:T(8,128)(2,1)S(1)} %collective-permute-done.17.refs_3_, ...), custom_call_target="tpu_custom_call", output_to_operand_aliasing={{}: (6, {})} | custom-call | flops 1 | bytes 1 | tf_op jit(solution)/shard_map/pallas_call | solution.py:181
  (39 shorter events, 4.4 us)
Async XLA Ops:
  0.0 32.4 %copy-start = (bf16[512,2048]{1,0:T(8,128)(2,1)S(1)}, bf16[512,2048]{1,0:T(8,128)(2,1)}, u32[]{:S(2)}) copy-start(bf16[512,2048]{1,0:T(8,128)(2,1)} %refs_0_.1) | copy-start | bytes 6291460
  0.0 4.9 %copy-start.4 = (bf16[512,1024]{1,0:T(8,128)(2,1)S(1)}, bf16[512,1024]{1,0:T(8,128)(2,1)}, u32[]{:S(2)}) copy-start(bf16[512,1024]{1,0:T(8,128)(2,1)} %param.5) | copy-start | bytes 3145732
  0.0 52.1 %copy-start.5 = (bf16[1024,128]{1,0:T(8,128)(2,1)S(1)}, bf16[1024,128]{1,0:T(8,128)(2,1)}, u32[]{:S(2)}) copy-start(bf16[1024,128]{1,0:T(8,128)(2,1)} %param.7) | copy-start | bytes 786436
  1.8 15.8 %collective-permute-start.9 = (bf16[512,512]{1,0:T(8,128)(2,1)S(1)}, bf16[512,512]{1,0:T(8,128)(2,1)S(1)}, u32[]{:S(2)}, u32[]{:S(2)}) collective-permute-start(bf16[512,512]{1,0:T(8,128)(2,1)S(1)} %get-tuple-element.40), channel_id=1, source_target_pairs={{0,8},{4,12},{8,0},{12,4},{1,9},{5,13},{9,1},{13,5},{2,10},{6,14},... | collective-permute-start | bytes 1572872 | tf_op jit(solution)/shard_map/ppermute | solution.py:211
  5.0 14.9 %collective-permute-start.7 = (bf16[512,512]{1,0:T(8,128)(2,1)S(1)}, bf16[512,512]{1,0:T(8,128)(2,1)S(1)}, u32[]{:S(2)}, u32[]{:S(2)}) collective-permute-start(bf16[512,512]{1,0:T(8,128)(2,1)S(1)} %get-tuple-element.43.refs_14_), channel_id=1, source_target_pairs={{0,1},{1,0},{2,3},{3,2},{4,5},{5,4},{6,7},{7,6},{8,9},{9,8},{10,11... | collective-permute-start | bytes 1572872 | tf_op jit(solution)/shard_map/ppermute | solution.py:208
  6.6 13.3 %collective-permute-start.8 = (bf16[512,512]{1,0:T(8,128)(2,1)S(1)}, bf16[512,512]{1,0:T(8,128)(2,1)S(1)}, u32[]{:S(2)}, u32[]{:S(2)}) collective-permute-start(bf16[512,512]{1,0:T(8,128)(2,1)S(1)} %get-tuple-element.43.refs_14_), channel_id=1, source_target_pairs={{1,2},{2,1},{5,6},{6,5},{9,10},{10,9},{13,14},{14,13},{17,18},{18,... | collective-permute-start | bytes 1572872 | tf_op jit(solution)/shard_map/ppermute | solution.py:208
  7.3 20.7 %collective-permute-start.3 = (bf16[512,512]{1,0:T(8,128)(2,1)S(1)}, bf16[512,512]{1,0:T(8,128)(2,1)S(1)}, u32[]{:S(2)}, u32[]{:S(2)}) collective-permute-start(bf16[512,512]{1,0:T(8,128)(2,1)S(1)} %get-tuple-element.42), channel_id=1, source_target_pairs={{0,8},{4,12},{8,0},{12,4},{1,9},{5,13},{9,1},{13,5},{2,10},{6,14},... | collective-permute-start | bytes 1572872 | tf_op jit(solution)/shard_map/ppermute | solution.py:211
  7.9 23.2 %collective-permute-start.1 = (bf16[512,512]{1,0:T(8,128)(2,1)S(1)}, bf16[512,512]{1,0:T(8,128)(2,1)S(1)}, u32[]{:S(2)}, u32[]{:S(2)}) collective-permute-start(bf16[512,512]{1,0:T(8,128)(2,1)S(1)} %get-tuple-element.44.refs_10_), channel_id=1, source_target_pairs={{0,1},{1,0},{2,3},{3,2},{4,5},{5,4},{6,7},{7,6},{8,9},{9,8},{10,11... | collective-permute-start | bytes 1572872 | tf_op jit(solution)/shard_map/ppermute | solution.py:208
  17.6 13.5 %collective-permute-start.2 = (bf16[512,512]{1,0:T(8,128)(2,1)S(1)}, bf16[512,512]{1,0:T(8,128)(2,1)S(1)}, u32[]{:S(2)}, u32[]{:S(2)}) collective-permute-start(bf16[512,512]{1,0:T(8,128)(2,1)S(1)} %get-tuple-element.44.refs_10_), channel_id=1, source_target_pairs={{1,2},{2,1},{5,6},{6,5},{9,10},{10,9},{13,14},{14,13},{17,18},{18,... | collective-permute-start | bytes 1572872 | tf_op jit(solution)/shard_map/ppermute | solution.py:208
  19.9 22.5 %collective-permute-start.10 = (bf16[512,512]{1,0:T(8,128)(2,1)S(1)}, bf16[512,512]{1,0:T(8,128)(2,1)S(1)}, u32[]{:S(2)}, u32[]{:S(2)}) collective-permute-start(bf16[512,512]{1,0:T(8,128)(2,1)S(1)} %collective-permute-done.8.refs_16_), channel_id=1, source_target_pairs={{1,0},{2,3},{5,4},{6,7},{9,8},{10,11},{13,12},{14,15},{17,16},{18,... | collective-permute-start | bytes 1572872 | tf_op jit(solution)/shard_map/ppermute | solution.py:208
  21.2 21.9 %collective-permute-start.11 = (bf16[512,512]{1,0:T(8,128)(2,1)S(1)}, bf16[512,512]{1,0:T(8,128)(2,1)S(1)}, u32[]{:S(2)}, u32[]{:S(2)}) collective-permute-start(bf16[512,512]{1,0:T(8,128)(2,1)S(1)} %collective-permute-done.7.refs_15_), channel_id=1, source_target_pairs={{1,2},{2,1},{5,6},{6,5},{9,10},{10,9},{13,14},{14,13},{17,18},{18,... | collective-permute-start | bytes 1572872 | tf_op jit(solution)/shard_map/ppermute | solution.py:208
  28.0 15.2 %collective-permute-start.12 = (bf16[512,512]{1,0:T(8,128)(2,1)S(1)}, bf16[512,512]{1,0:T(8,128)(2,1)S(1)}, u32[]{:S(2)}, u32[]{:S(2)}) collective-permute-start(bf16[512,512]{1,0:T(8,128)(2,1)S(1)} %get-tuple-element.30), channel_id=1, source_target_pairs={{0,8},{4,12},{8,0},{12,4},{1,9},{5,13},{9,1},{13,5},{2,10},{6,14},... | collective-permute-start | bytes 1572872 | tf_op jit(solution)/shard_map/ppermute | solution.py:211
  31.1 21.0 %collective-permute-start.4 = (bf16[512,512]{1,0:T(8,128)(2,1)S(1)}, bf16[512,512]{1,0:T(8,128)(2,1)S(1)}, u32[]{:S(2)}, u32[]{:S(2)}) collective-permute-start(bf16[512,512]{1,0:T(8,128)(2,1)S(1)} %collective-permute-done.2.refs_12_), channel_id=1, source_target_pairs={{1,0},{2,3},{5,4},{6,7},{9,8},{10,11},{13,12},{14,15},{17,16},{18,... | collective-permute-start | bytes 1572872 | tf_op jit(solution)/shard_map/ppermute | solution.py:208
  32.4 26.7 %collective-permute-start = (bf16[512,2048]{1,0:T(8,128)(2,1)S(1)}, bf16[512,2048]{1,0:T(8,128)(2,1)S(1)}, u32[]{:S(2)}, u32[]{:S(2)}) collective-permute-start(bf16[512,2048]{1,0:T(8,128)(2,1)S(1)} %copy-done), channel_id=1, source_target_pairs={{0,4},{4,0},{8,12},{12,8},{1,5},{5,1},{9,13},{13,9},{2,6},{6,2},{1... | collective-permute-start | bytes 6291464 | tf_op jit(solution)/shard_map/ppermute | solution.py:211
  42.3 9.9 %collective-permute-start.5 = (bf16[512,512]{1,0:T(8,128)(2,1)S(1)}, bf16[512,512]{1,0:T(8,128)(2,1)S(1)}, u32[]{:S(2)}, u32[]{:S(2)}) collective-permute-start(bf16[512,512]{1,0:T(8,128)(2,1)S(1)} %collective-permute-done.1.refs_11_), channel_id=1, source_target_pairs={{1,2},{2,1},{5,6},{6,5},{9,10},{10,9},{13,14},{14,13},{17,18},{18,... | collective-permute-start | bytes 1572872 | tf_op jit(solution)/shard_map/ppermute | solution.py:208
  43.0 11.1 %collective-permute-start.6 = (bf16[512,512]{1,0:T(8,128)(2,1)S(1)}, bf16[512,512]{1,0:T(8,128)(2,1)S(1)}, u32[]{:S(2)}, u32[]{:S(2)}) collective-permute-start(bf16[512,512]{1,0:T(8,128)(2,1)S(1)} %get-tuple-element.25), channel_id=1, source_target_pairs={{0,8},{4,12},{8,0},{12,4},{1,9},{5,13},{9,1},{13,5},{2,10},{6,14},... | collective-permute-start | bytes 1572872 | tf_op jit(solution)/shard_map/ppermute | solution.py:211
  43.2 10.9 %collective-permute-start.15 = (bf16[512,512]{1,0:T(8,128)(2,1)S(1)}, bf16[512,512]{1,0:T(8,128)(2,1)S(1)}, u32[]{:S(2)}, u32[]{:S(2)}) collective-permute-start(bf16[512,512]{1,0:T(8,128)(2,1)S(1)} %collective-permute-done.9.refs_4_), channel_id=1, source_target_pairs={{0,4},{4,0},{8,12},{12,8},{1,5},{5,1},{9,13},{13,9},{2,6},{6,2},{1... | collective-permute-start | bytes 1572872 | tf_op jit(solution)/shard_map/ppermute | solution.py:211
  52.1 3.3 %collective-permute-start.13 = (bf16[512,512]{1,0:T(8,128)(2,1)S(1)}, bf16[512,512]{1,0:T(8,128)(2,1)S(1)}, u32[]{:S(2)}, u32[]{:S(2)}) collective-permute-start(bf16[512,512]{1,0:T(8,128)(2,1)S(1)} %collective-permute-done.3.refs_2_), channel_id=1, source_target_pairs={{0,4},{4,0},{8,12},{12,8},{1,5},{5,1},{9,13},{13,9},{2,6},{6,2},{1... | collective-permute-start | bytes 1572872 | tf_op jit(solution)/shard_map/ppermute | solution.py:211
  52.3 6.9 %collective-permute-start.16 = (bf16[512,512]{1,0:T(8,128)(2,1)S(1)}, bf16[512,512]{1,0:T(8,128)(2,1)S(1)}, u32[]{:S(2)}, u32[]{:S(2)}) collective-permute-start(bf16[512,512]{1,0:T(8,128)(2,1)S(1)} %collective-permute-done.12.refs_5_), channel_id=1, source_target_pairs={{0,4},{4,0},{8,12},{12,8},{1,5},{5,1},{9,13},{13,9},{2,6},{6,2},{1... | collective-permute-start | bytes 1572872 | tf_op jit(solution)/shard_map/ppermute | solution.py:211
  54.1 5.0 %collective-permute-start.14 = (bf16[512,512]{1,0:T(8,128)(2,1)S(1)}, bf16[512,512]{1,0:T(8,128)(2,1)S(1)}, u32[]{:S(2)}, u32[]{:S(2)}) collective-permute-start(bf16[512,512]{1,0:T(8,128)(2,1)S(1)} %collective-permute-done.6.refs_3_), channel_id=1, source_target_pairs={{0,4},{4,0},{8,12},{12,8},{1,5},{5,1},{9,13},{13,9},{2,6},{6,2},{1... | collective-permute-start | bytes 1572872 | tf_op jit(solution)/shard_map/ppermute | solution.py:211
  54.1 18.4 %collective-permute-start.18 = (bf16[512,512]{1,0:T(8,128)(2,1)S(1)}, bf16[512,512]{1,0:T(8,128)(2,1)S(1)}, u32[]{:S(2)}, u32[]{:S(2)}) collective-permute-start(bf16[512,512]{1,0:T(8,128)(2,1)S(1)} %collective-permute-done.5.refs_2_), channel_id=1, source_target_pairs={{1,0},{2,3},{5,4},{6,7},{9,8},{10,11},{13,12},{14,15},{17,16},{18,... | collective-permute-start | bytes 1572872 | tf_op jit(solution)/shard_map/ppermute | solution.py:208
  55.4 27.0 %collective-permute-start.17 = (bf16[512,512]{1,0:T(8,128)(2,1)S(1)}, bf16[512,512]{1,0:T(8,128)(2,1)S(1)}, u32[]{:S(2)}, u32[]{:S(2)}) collective-permute-start(bf16[512,512]{1,0:T(8,128)(2,1)S(1)} %collective-permute-done.11.refs_2_), channel_id=1, source_target_pairs={{1,0},{2,3},{5,4},{6,7},{9,8},{10,11},{13,12},{14,15},{17,16},{18,... | collective-permute-start | bytes 1572872 | tf_op jit(solution)/shard_map/ppermute | solution.py:208
  72.5 2.2 %copy-start.2 = (f32[512,2048]{1,0:T(8,128)S(1)}, f32[512,2048]{1,0:T(8,128)}, u32[]{:S(2)}) copy-start(f32[512,2048]{1,0:T(8,128)} %get-tuple-element.37.refs_0_) | copy-start | bytes 12582916
  74.7 7.7 %copy-start.1 = (f32[512,2048]{1,0:T(8,128)S(1)}, f32[512,2048]{1,0:T(8,128)}, u32[]{:S(2)}) copy-start(f32[512,2048]{1,0:T(8,128)} %get-tuple-element.34.refs_0_) | copy-start | bytes 12582916
  (2 other events, 2.1 us)

commit v3 on v2

v3 whole, which is shorter than its diff:
```python
import functools
import math

import jax
import jax.numpy as jnp
from jax import lax
from jax.experimental import pallas as pl
from jax.experimental.pallas import tpu as pltpu
from jax.sharding import PartitionSpec as P

CH = 32
LANES = 128
GROUP = LANES // CH
CORES = 2
FIRST_PART, PART_UNITS = 1, 2
CROSS_PARTS = (4, 3, 1)
EARLY_VMEM = 28 * 2**20
LATE_VMEM = 16 * 2**20


def spread_weights(w_out):
    pair = w_out.shape[1]
    by_e = w_out.reshape(CH, CH, pair).transpose(1, 0, 2)
    same = jnp.eye(GROUP, dtype=jnp.bool_)[None, :, None, :, None]
    full = jnp.where(same, by_e[:, None, :, None, :], jnp.zeros((), w_out.dtype))
    return full.reshape(CH * LANES, GROUP * pair)


def turned(right, perm):
    return lax.dot_general(perm, right, (((1,), (1,)), ((), ())), preferred_element_type=jnp.float32).astype(
        jnp.bfloat16
    )


def regroup(cols):
    res = cols // CH
    to = lax.broadcasted_iota(jnp.int32, (cols, cols), 0)
    source = lax.broadcasted_iota(jnp.int32, (cols, cols), 1)
    return jnp.where(source == (to % res) * CH + to // res, 1.0, 0.0).astype(jnp.bfloat16)


def early_kernel(places, *refs):
    nl = len(places)
    lefts = refs[:nl]
    own, beside, middle, opposite = refs[nl : nl + 4]
    sums = refs[nl + 4 : -4]
    late_ref, left_v, rt, sem = refs[-4:]
    l, r = lax.axis_index("left"), lax.axis_index("right")
    end = jnp.logical_or(l == 0, l == 3)
    rows = left_v.shape[0] // 3
    flip = 1 - 2 * (r % 2)
    far = (r + 2) % 4
    owners = (r, r + flip, far, far + flip)

    copies = []
    for n, (k, row) in enumerate(places):
        s = owners[k]
        odd = (s + l) % 2
        slot = jnp.where(s // 2 == l // 2, odd, 3 - odd)
        height = lefts[n].shape[0]
        at = pl.multiple_of(jnp.minimum(slot, 2) * rows + row, math.gcd(rows, row))
        late = late_ref.at[row : row + height, :]

        @pl.when(slot < 3)
        def _():
            pltpu.make_async_copy(lefts[n], left_v.at[pl.ds(at, height), :], sem.at[n]).start()

        @pl.when(slot == 3)
        def _():
            pltpu.make_async_copy(lefts[n], late, sem.at[n]).start()

        copies.append(pltpu.make_async_copy(lefts[n], late, sem.at[n]))

    first_row = 0
    for total in sums:
        cols = total.shape[0]
        perm = regroup(cols)
        here = pl.ds(first_row, cols)
        rt[here, :rows] = turned(own[:, here], perm)
        rt[here, rows : 2 * rows] = turned(beside[:, here], perm)

        @pl.when(end)
        def _():
            rt[here, 2 * rows :] = turned(opposite[:, here], perm)

        @pl.when(jnp.logical_not(end))
        def _():
            rt[here, 2 * rows :] = turned(middle[:, here], perm)

        first_row += cols
    for copy in copies:
        copy.wait()
    first_row = 0
    for total in sums:
        cols = total.shape[0]
        total[...] = jnp.dot(rt[first_row : first_row + cols, :], left_v[...], preferred_element_type=jnp.float32)
        first_row += cols


def early_sums(places, lefts, rights, cols):
    rows, width = lefts[0].shape
    vmem = pl.BlockSpec(memory_space=pltpu.VMEM)
    anywhere = pl.BlockSpec(memory_space=pl.ANY)
    parts = len(cols)
    out = pl.pallas_call(
        functools.partial(early_kernel, places),
        out_shape=[jax.ShapeDtypeStruct((c, width), jnp.float32) for c in cols]
        + [jax.ShapeDtypeStruct((rows, width), jnp.bfloat16)],
        in_specs=[anywhere] * len(lefts) + [vmem] * 4,
        out_specs=[vmem] * parts + [anywhere],
        scratch_shapes=[
            pltpu.VMEM((3 * rows, width), jnp.bfloat16),
            pltpu.VMEM((sum(cols), 3 * rows), jnp.bfloat16),
            pltpu.SemaphoreType.DMA((len(lefts),)),
        ],
        compiler_params=pltpu.CompilerParams(vmem_limit_bytes=EARLY_VMEM),
        cost_estimate=pl.CostEstimate(flops=1, bytes_accessed=1, transcendentals=0),
    )(*lefts, *rights)
    return out[:parts], out[parts]


def late_kernel(line, start, *refs):
    if line:
        sums, left, right, wide, counts = refs[:5]
    else:
        left, right, wide, counts = refs[:4]
    out_ref, rt, lhs, out_v, sem = refs[-5:]
    width = left.shape[1]
    res = right.shape[1] // CH
    rt[...] = turned(right[...], regroup(right.shape[1]))
    total = jnp.dot(rt[...], left[...], preferred_element_type=jnp.float32)
    if line:
        total += sums[...]
    outer = total.astype(jnp.bfloat16)
    for g in range(width // LANES):
        for e in range(CH):
            lhs[g * res : (g + 1) * res, e * LANES : (e + 1) * LANES] = outer[
                e * res : (e + 1) * res, g * LANES : (g + 1) * LANES
            ]
    projected = jnp.dot(lhs[...], wide[...], preferred_element_type=jnp.float32)
    pair = out_v.shape[2]
    for g in range(width // LANES):
        for i in range(GROUP):
            row = g * GROUP + i
            out_v[row] = projected[g * res : (g + 1) * res, i * pair : (i + 1) * pair] / counts[:, row : row + 1]
    out_copy = pltpu.make_async_copy(out_v, out_ref.at[:, pl.ds(start, res), :], sem)
    out_copy.start()
    out_copy.wait()


def pair_features(line, start, operands, counts, right_dev, before):
    vmem = pl.BlockSpec(memory_space=pltpu.VMEM)
    anywhere = pl.BlockSpec(memory_space=pl.ANY)
    left, right, wide = operands[-3:]
    rows, width = left.shape
    cols = right.shape[1]
    res, left_dev = cols // CH, width // CH
    pair = wide.shape[1] // GROUP
    operands = [*operands, counts]
    specs = [vmem] * len(operands)
    aliases = {}
    if before is not None:
        aliases = {len(operands): 0}
        operands.append(before)
        specs.append(anywhere)
    return pl.pallas_call(
        functools.partial(late_kernel, line, start),
        out_shape=jax.ShapeDtypeStruct((left_dev, right_dev, pair), jnp.float32),
        in_specs=specs,
        out_specs=anywhere,
        input_output_aliases=aliases,
        scratch_shapes=[
            pltpu.VMEM((cols, rows), jnp.bfloat16),
            pltpu.VMEM((width // LANES * res, CH * LANES), jnp.bfloat16),
            pltpu.VMEM((left_dev, res, pair), jnp.float32),
            pltpu.SemaphoreType.DMA,
        ],
        compiler_params=pltpu.CompilerParams(vmem_limit_bytes=LATE_VMEM if line else 2 * LATE_VMEM),
        cost_estimate=pl.CostEstimate(flops=1, bytes_accessed=1, transcendentals=0),
    )(*operands)


def gather_line(left_act, right_act, wide):
    cut = right_act.shape[1] * FIRST_PART // PART_UNITS
    end = lax.axis_index("left") % 3 == 0

    def hop(x, pairs):
        return lax.ppermute(x, "left", pairs)

    def partner(x, step):
        return lax.ppermute(x, "right", [(i, i ^ step) for i in range(4)])

    def last(cols, *arrived):
        inward = end
        for x in arrived:
            same = x[: right_act.shape[0], : cut]
            inward = jnp.logical_and(inward, same == same)
        return hop(jnp.where(inward, right_act[:, cols], middle[:, cols]), ((0, 2), (3, 1), (1, 0), (2, 3)))

    far = partner(left_act, CORES)
    near = partner(left_act, 1)
    beside = hop(right_act, [(i, i ^ 1) for i in range(4)])
    middle = hop(right_act, ((1, 2), (2, 1)))
    opposite = hop(right_act, ((0, 3), (3, 0)))
    late = (last(slice(0, cut), near, beside), last(slice(cut, None), wide))
    unit = far.shape[0] // sum(CROSS_PARTS)
    starts = [sum(CROSS_PARTS[:n]) * unit for n in range(len(CROSS_PARTS))]
    cross = [partner(far[n : n + h * unit], 1) for n, h in zip(starts, CROSS_PARTS)]
    lefts = [left_act, near, far, *cross]
    places = [(0, 0), (1, 0), (2, 0)] + [(3, n) for n in starts]
    return places, lefts, (right_act, beside, middle, opposite), late


def shards(line, left_act, right_act, counts, w_out):
    right_dev = counts.shape[1]
    cut = right_dev * FIRST_PART // PART_UNITS
    by_right = counts.astype(jnp.float32).T
    count_parts = (by_right[:cut], by_right[cut:])
    wide = spread_weights(w_out)
    if line:
        places, lefts, early, late = gather_line(left_act, right_act, wide)
        sums, left_late = early_sums(places, lefts, early, [x.shape[1] for x in late])
        operands = [(sums[p], left_late, late[p], wide) for p in range(2)]
    else:
        left_full = lax.all_gather(left_act, "right", axis=0, tiled=True)
        full = lax.all_gather(right_act, "left", axis=0, tiled=True)
        operands = [(left_full, x, wide) for x in (full[:, : cut * CH], full[:, cut * CH :])]
    out = None
    for start, given, count in zip((0, cut), operands, count_parts):
        out = pair_features(line, start, given, count, right_dev, out)
    return out


def solution(mesh):
    in_specs = (
        P(("groups", "right"), "left"),
        P(("groups", "left"), "right"),
        P(("groups", "left"), "right"),
        P(),
    )
    out_specs = P(("groups", "left"), "right", None)
    line = mesh.shape["left"] == 4 and mesh.shape["right"] == 4
    body = functools.partial(shards, line)
    return jax.shard_map(body, mesh=mesh, in_specs=in_specs, out_specs=out_specs, check_vma=False)
```

time: 86.7 us -> 84.8 us (0.978)
  waiting for transfers between devices: 38.2 us -> 42.5 us
  local copies, waits for them, and re-layouts: 6.29 us -> 2.02 us
  starting transfers between devices: 20 us -> 17.4 us
  other arithmetic: 1.62 us -> 3.87 us
  Pallas kernels: 19.7 us -> 18.3 us
    ppermute x9 -> x5, waiting for transfers between devices: 12.9 us -> 37.2 us  [partner(): return lax.ppermute(x, 'right', [(i, i ^ step) for i in range(4)])]
    ppermute x10 -> x5, waiting for transfers between devices: 25.4 us -> 5.36 us  [hop(): return lax.ppermute(x, 'left', pairs)]
    unnamed x15 -> x7, local copies, waits for them, and re-layouts: 4.29 us -> 0.83 us
    ppermute x9 -> x5, starting transfers between devices: 6.16 us -> 3.67 us  [partner(): return lax.ppermute(x, 'right', [(i, i ^ step) for i in range(4)])]
    select_n x0 -> x1, other arithmetic: none -> 1.83 us  [last(): jnp.where(inward, right_act[:, cols], middle[:, cols])]
    slice x2 -> x3, local copies, waits for them, and re-layouts: 1.89 us -> 0.14 us  [gather_line(): far[n:n + h * unit]]
    transpose x1, local copies, waits for them, and re-layouts: 0.1 us -> 1.06 us  [spread_weights(): by_e = w_out.reshape(CH, CH, pair).transpose(1, 0, 2)]
    ppermute x10 -> x5, starting transfers between devices: 13.9 us -> 13.8 us  [hop(): return lax.ppermute(x, 'left', pairs)]
  transfers between devices with their start and end apart: 19 -> 10, of which waited for: 8 -> 3; matrix products, arithmetic and copies ran while one was open for 3% -> 7% of each run, Pallas kernels for 18% -> 18%
where the time goes in v3:
time: 84.8 us; the launch traced here: 84.5 us
  waiting for transfers between devices  42.5 us (50%)
  Pallas kernels  18.3 us (22%)
  starting transfers between devices  17.4 us (21%)
  other arithmetic  3.87 us (5%)
  local copies, waits for them, and re-layouts  2.02 us (2%)
    ppermute x5, waiting for transfers between devices, partner(): return lax.ppermute(x, 'right', [(i, i ^ step) for i in range(4)])  37.2 us
    ppermute x5, starting transfers between devices, hop(): return lax.ppermute(x, 'left', pairs)  13.8 us
    pallas_call x1, Pallas kernels, early_sums(): pl.pallas_call(functools.partial(early_kernel, places), out_shape=[jax.Sh...  11.4 us
    pallas_call x2, Pallas kernels, pair_features(): pl.pallas_call(functools.partial(late_kernel, line, start), out_shape=jax...  6.92 us
    ppermute x5, waiting for transfers between devices, hop(): return lax.ppermute(x, 'left', pairs)  5.36 us
    ppermute x5, starting transfers between devices, partner(): return lax.ppermute(x, 'right', [(i, i ^ step) for i in range(4)])  3.67 us
    select_n x1, other arithmetic, last(): jnp.where(inward, right_act[:, cols], middle[:, cols])  1.83 us
  transfers between devices with their start and end apart: 10, of which 3 were waited for; matrix products, arithmetic and copies ran while one was open for 7% of the time, Pallas kernels for 18%

profile of v3, /device:TPU:0, one launch (start us, length us, event | category | flops | bytes accessed | tf_op | source)
XLA Modules:
  0.0 84.5 jit_solution(13906243150792547272)
XLA Ops:
  0.0 3.0 %collective-permute-start.1 = (bf16[512,2048]{1,0:T(8,128)(2,1)}, bf16[512,2048]{1,0:T(8,128)(2,1)S(1)}, u32[]{:S(2)}, u32[]{:S(2)}) collective-permute-start(bf16[512,2048]{1,0:T(8,128)(2,1)} %refs_0_.1), channel_id=1, source_target_pairs={{0,8},{4,12},{8,0},{12,4},{1,9},{5,13},{9,1},{13,5},{2,10},{6,14},... | collective-permute-start | bytes 6291464 | tf_op jit(solution)/shard_map/ppermute | solution.py:191
  3.0 1.6 %collective-permute-start.5 = (bf16[512,1024]{1,0:T(8,128)(2,1)}, bf16[512,1024]{1,0:T(8,128)(2,1)}, u32[]{:S(2)}, u32[]{:S(2)}) collective-permute-start(bf16[512,1024]{1,0:T(8,128)(2,1)} %refs_6_.1), channel_id=1, source_target_pairs={{0,1},{1,0},{2,3},{3,2},{4,5},{5,4},{6,7},{7,6},{8,9},{9,8},{10,11... | collective-permute-start | bytes 3145736 | tf_op jit(solution)/shard_map/ppermute | solution.py:188
  4.5 0.7 collective-permute-start.6
  5.3 4.4 %collective-permute-start.7 = (bf16[512,1024]{1,0:T(8,128)(2,1)}, bf16[512,1024]{1,0:T(8,128)(2,1)}, u32[]{:S(2)}, u32[]{:S(2)}) collective-permute-start(bf16[512,1024]{1,0:T(8,128)(2,1)} %refs_6_.1), channel_id=1, source_target_pairs={{0,3},{3,0},{4,7},{7,4},{8,11},{11,8},{12,15},{15,12},{16,19},{19,... | collective-permute-start | bytes 3145736 | tf_op jit(solution)/shard_map/ppermute | solution.py:188
  9.7 1.1 %copy.6 = bf16[32,32,128]{2,1,0:T(8,128)(2,1)S(1)} copy(bf16[32,32,128]{2,0,1:T(8,128)(2,1)} %bitcast.18) | data formatting | bytes 524288 | tf_op jit(solution)/shard_map/transpose | solution.py:23
  10.8 0.0 copy-start
  10.8 1.6 %broadcast_select_fusion = bf16[32,4,32,4,128]{4,3,2,1,0:T(4,128)(2,1)S(1)} fusion(pred[4,4]{1,0:T(4,128)(4,1)S(1)} %iota_compare_fusion, bf16[32,32,128]{2,1,0:T(8,128)(2,1)S(1)} %copy.6), kind=kLoop, calls=%fused_computation.1 | loop fusion | flops 2097152 | bytes 4456464 | tf_op jit(solution)/shard_map/jit(_where)/select_n | solution.py:25
  12.4 36.4 %collective-permute-done.1.refs_2_ = bf16[512,2048]{1,0:T(8,128)(2,1)S(1)} collective-permute-done((bf16[512,2048]{1,0:T(8,128)(2,1)}, bf16[512,2048]{1,0:T(8,128)(2,1)S(1)}, u32[]{:S(2)}, u32[]{:S(2)}) %collective-permute-start.1) | collective-permute-done | bytes 2097184 | tf_op jit(solution)/shard_map/ppermute | solution.py:191
  48.8 0.1 slice.49
  48.9 0.1 collective-permute-start.2
  49.0 0.4 compare_and_fusion
  49.4 0.1 slice.50
  49.5 0.6 collective-permute-start.3
  50.0 1.8 %and_select_fusion = (bf16[512,512]{1,0:T(8,128)(2,1)S(1)}, bf16[512,512]{1,0:T(8,128)(2,1)S(1)}) fusion(bf16[512,1024]{1,0:T(8,128)(2,1)S(1)} %collective-permute-done.6.refs_8_, bf16[512,1024]{1,0:T(8,128)(2,1)} %collective-permute-done.5.refs_7_, bf16[512,2048]{1,0:T(8,128)(2,1)} %collective-permute-done.refs_1_, bf16[512,1024]{1,0:T(8,128)(2,1)S(1)} %copy-done, ...), kind=kLoop, calls=%fused_computation.3 | loop fusion | flops 2097152 | bytes 4456449 | tf_op jit(solution)/shard_map/jit(_where)/select_n | solution.py:198
  51.9 7.0 %collective-permute-start.9 = (bf16[512,512]{1,0:T(8,128)(2,1)S(1)}, bf16[512,512]{1,0:T(8,128)(2,1)S(1)}, u32[]{:S(2)}, u32[]{:S(2)}) collective-permute-start(bf16[512,512]{1,0:T(8,128)(2,1)S(1)} %get-tuple-element.11), channel_id=1, source_target_pairs={{0,2},{3,1},{1,0},{2,3},{4,6},{7,5},{5,4},{6,7},{8,10},{11,9},{9,8... | collective-permute-start | bytes 1572872 | tf_op jit(solution)/shard_map/ppermute | solution.py:188
  58.9 0.1 collective-permute-start.8
  59.0 0.1 collective-permute-start.4
  59.1 0.7 copy.11
  59.8 0.7 collective-permute-done.4.refs_5_
  60.6 0.1 copy-done.1
  60.7 11.4 %shard_map.46 = (f32[512,2048]{1,0:T(8,128)S(1)}, f32[512,2048]{1,0:T(8,128)S(1)}, bf16[512,2048]{1,0:T(8,128)(2,1)S(1)}) custom-call(bf16[512,2048]{1,0:T(8,128)(2,1)S(1)} %copy-done.1, bf16[512,2048]{1,0:T(8,128)(2,1)} %collective-permute-done.refs_1_, bf16[512,2048]{1,0:T(8,128)(2,1)S(1)} %collective-permute-done.1.refs_2_, ...), custom_call_target="tpu_custom_call" | custom-call | flops 1 | bytes 1 | tf_op jit(solution)/shard_map/pallas_call | solution.py:105
  72.1 3.5 %shard_map.47.refs_5_ = f32[64,32,128]{2,1,0:T(8,128)} custom-call(f32[512,2048]{1,0:T(8,128)S(1)} %get-tuple-element.10.refs_0_, bf16[512,2048]{1,0:T(8,128)(2,1)S(1)} %get-tuple-element.9.refs_1_, bf16[512,512]{1,0:T(8,128)(2,1)S(1)} %collective-permute-done.9.refs_2_, bf16[4096,512]{1,0:T(8,128)(2,1)S(1)} %bitcast.14, f32[16,64]{1,0:T(8,128)S(1)} %get-tuple-element.13.refs_4_), custom_call_target="tpu_custom_call" | custom-call | flops 1 | bytes 1 | tf_op jit(solution)/shard_map/pallas_call | solution.py:166
  75.5 5.4 %collective-permute-done.8.refs_2_ = bf16[512,512]{1,0:T(8,128)(2,1)S(1)} collective-permute-done((bf16[512,512]{1,0:T(8,128)(2,1)S(1)}, bf16[512,512]{1,0:T(8,128)(2,1)S(1)}, u32[]{:S(2)}, u32[]{:S(2)}) %collective-permute-start.8) | collective-permute-done | bytes 524320 | tf_op jit(solution)/shard_map/ppermute | solution.py:188
  80.9 3.5 %shard_map.48 = f32[64,32,128]{2,1,0:T(8,128)} custom-call(f32[512,2048]{1,0:T(8,128)S(1)} %get-tuple-element.8.refs_0_, bf16[512,2048]{1,0:T(8,128)(2,1)S(1)} %get-tuple-element.9.refs_1_, bf16[512,512]{1,0:T(8,128)(2,1)S(1)} %collective-permute-done.8.refs_2_, bf16[4096,512]{1,0:T(8,128)(2,1)S(1)} %bitcast.15, ...), custom_call_target="tpu_custom_call", output_to_operand_aliasing={{}: (5, {})} | custom-call | flops 1 | bytes 1 | tf_op jit(solution)/shard_map/pallas_call | solution.py:166
  (16 shorter events, 0.1 us)
Async XLA Ops:
  0.0 48.8 %collective-permute-start.1 = (bf16[512,2048]{1,0:T(8,128)(2,1)}, bf16[512,2048]{1,0:T(8,128)(2,1)S(1)}, u32[]{:S(2)}, u32[]{:S(2)}) collective-permute-start(bf16[512,2048]{1,0:T(8,128)(2,1)} %refs_0_.1), channel_id=1, source_target_pairs={{0,8},{4,12},{8,0},{12,4},{1,9},{5,13},{9,1},{13,5},{2,10},{6,14},... | collective-permute-start | bytes 6291464 | tf_op jit(solution)/shard_map/ppermute | solution.py:191
  3.0 47.1 %collective-permute-start = (bf16[512,2048]{1,0:T(8,128)(2,1)}, bf16[512,2048]{1,0:T(8,128)(2,1)}, u32[]{:S(2)}, u32[]{:S(2)}) collective-permute-start(bf16[512,2048]{1,0:T(8,128)(2,1)} %refs_0_.1), channel_id=1, source_target_pairs={{0,4},{4,0},{8,12},{12,8},{1,5},{5,1},{9,13},{13,9},{2,6},{6,2},{1... | collective-permute-start | bytes 6291464 | tf_op jit(solution)/shard_map/ppermute | solution.py:191
  3.0 46.5 %collective-permute-start.5 = (bf16[512,1024]{1,0:T(8,128)(2,1)}, bf16[512,1024]{1,0:T(8,128)(2,1)}, u32[]{:S(2)}, u32[]{:S(2)}) collective-permute-start(bf16[512,1024]{1,0:T(8,128)(2,1)} %refs_6_.1), channel_id=1, source_target_pairs={{0,1},{1,0},{2,3},{3,2},{4,5},{5,4},{6,7},{7,6},{8,9},{9,8},{10,11... | collective-permute-start | bytes 3145736 | tf_op jit(solution)/shard_map/ppermute | solution.py:188
  4.5 45.5 %collective-permute-start.6 = (bf16[512,1024]{1,0:T(8,128)(2,1)}, bf16[512,1024]{1,0:T(8,128)(2,1)S(1)}, u32[]{:S(2)}, u32[]{:S(2)}) collective-permute-start(bf16[512,1024]{1,0:T(8,128)(2,1)} %refs_6_.1), channel_id=1, source_target_pairs={{1,2},{2,1},{5,6},{6,5},{9,10},{10,9},{13,14},{14,13},{17,18},{18,... | collective-permute-start | bytes 3145736 | tf_op jit(solution)/shard_map/ppermute | solution.py:188
  5.3 53.7 %collective-permute-start.7 = (bf16[512,1024]{1,0:T(8,128)(2,1)}, bf16[512,1024]{1,0:T(8,128)(2,1)}, u32[]{:S(2)}, u32[]{:S(2)}) collective-permute-start(bf16[512,1024]{1,0:T(8,128)(2,1)} %refs_6_.1), channel_id=1, source_target_pairs={{0,3},{3,0},{4,7},{7,4},{8,11},{11,8},{12,15},{15,12},{16,19},{19,... | collective-permute-start | bytes 3145736 | tf_op jit(solution)/shard_map/ppermute | solution.py:188
  10.8 39.3 %copy-start = (bf16[512,1024]{1,0:T(8,128)(2,1)S(1)}, bf16[512,1024]{1,0:T(8,128)(2,1)}, u32[]{:S(2)}) copy-start(bf16[512,1024]{1,0:T(8,128)(2,1)} %refs_6_.1) | copy-start | bytes 3145732
  48.9 10.2 %copy-start.2 = (s32[64,32]{0,1:T(8,128)S(1)}, s32[64,32]{0,1:T(8,128)}, u32[]{:S(2)}) copy-start(s32[64,32]{0,1:T(8,128)} %param.6) | copy-start | bytes 24580
  48.9 11.7 %collective-permute-start.2 = (bf16[256,2048]{1,0:T(8,128)(2,1)S(1)}, bf16[256,2048]{1,0:T(8,128)(2,1)S(1)}, u32[]{:S(2)}, u32[]{:S(2)}) collective-permute-start(bf16[256,2048]{1,0:T(8,128)(2,1)S(1)} %slice.49), channel_id=1, source_target_pairs={{0,4},{4,0},{8,12},{12,8},{1,5},{5,1},{9,13},{13,9},{2,6},{6,2},{1... | collective-permute-start | bytes 3145736 | tf_op jit(solution)/shard_map/ppermute | solution.py:191
  49.5 11.1 %collective-permute-start.3 = (bf16[192,2048]{1,0:T(8,128)(2,1)S(1)}, bf16[192,2048]{1,0:T(8,128)(2,1)S(1)}, u32[]{:S(2)}, u32[]{:S(2)}) collective-permute-start(bf16[192,2048]{1,0:T(8,128)(2,1)S(1)} %slice.50), channel_id=1, source_target_pairs={{0,4},{4,0},{8,12},{12,8},{1,5},{5,1},{9,13},{13,9},{2,6},{6,2},{1... | collective-permute-start | bytes 2359304 | tf_op jit(solution)/shard_map/ppermute | solution.py:191
  51.9 20.2 %collective-permute-start.9 = (bf16[512,512]{1,0:T(8,128)(2,1)S(1)}, bf16[512,512]{1,0:T(8,128)(2,1)S(1)}, u32[]{:S(2)}, u32[]{:S(2)}) collective-permute-start(bf16[512,512]{1,0:T(8,128)(2,1)S(1)} %get-tuple-element.11), channel_id=1, source_target_pairs={{0,2},{3,1},{1,0},{2,3},{4,6},{7,5},{5,4},{6,7},{8,10},{11,9},{9,8... | collective-permute-start | bytes 1572872 | tf_op jit(solution)/shard_map/ppermute | solution.py:188
  58.9 22.0 %collective-permute-start.8 = (bf16[512,512]{1,0:T(8,128)(2,1)S(1)}, bf16[512,512]{1,0:T(8,128)(2,1)S(1)}, u32[]{:S(2)}, u32[]{:S(2)}) collective-permute-start(bf16[512,512]{1,0:T(8,128)(2,1)S(1)} %get-tuple-element.12), channel_id=1, source_target_pairs={{0,2},{3,1},{1,0},{2,3},{4,6},{7,5},{5,4},{6,7},{8,10},{11,9},{9,8... | collective-permute-start | bytes 1572872 | tf_op jit(solution)/shard_map/ppermute | solution.py:188
  59.0 1.6 %collective-permute-start.4 = (bf16[64,2048]{1,0:T(8,128)(2,1)S(1)}, bf16[64,2048]{1,0:T(8,128)(2,1)S(1)}, u32[]{:S(2)}, u32[]{:S(2)}) collective-permute-start(bf16[64,2048]{1,0:T(8,128)(2,1)S(1)} %slice.51), channel_id=1, source_target_pairs={{0,4},{4,0},{8,12},{12,8},{1,5},{5,1},{9,13},{13,9},{2,6},{6,2},{1... | collective-permute-start | bytes 786440 | tf_op jit(solution)/shard_map/ppermute | solution.py:191
  59.1 1.6 %copy-start.1 = (bf16[512,2048]{1,0:T(8,128)(2,1)S(1)}, bf16[512,2048]{1,0:T(8,128)(2,1)}, u32[]{:S(2)}) copy-start(bf16[512,2048]{1,0:T(8,128)(2,1)} %refs_0_.1) | copy-start | bytes 6291460

commit v4 on v3

--- a/solution.py
+++ b/solution.py
@@ -202,7 +202,7 @@
     beside = hop(right_act, [(i, i ^ 1) for i in range(4)])
     middle = hop(right_act, ((1, 2), (2, 1)))
     opposite = hop(right_act, ((0, 3), (3, 0)))
-    late = (last(slice(0, cut), near, beside), last(slice(cut, None), wide))
+    late = (last(slice(0, cut), beside), last(slice(cut, None), wide))
     unit = far.shape[0] // sum(CROSS_PARTS)
     starts = [sum(CROSS_PARTS[:n]) * unit for n in range(len(CROSS_PARTS))]
     cross = [partner(far[n : n + h * unit], 1) for n, h in zip(starts, CROSS_PARTS)]

time: 84.8 us -> 84.5 us (level)
  no operation moved by 1% of the time
where the time goes in v4:
time: 84.5 us; the launch traced here: 84.2 us
  waiting for transfers between devices  42.5 us (50%)
  Pallas kernels  18.3 us (22%)
  starting transfers between devices  17.5 us (21%)
  other arithmetic  3.57 us (4%)
  local copies, waits for them, and re-layouts  2.02 us (2%)
    ppermute x5, waiting for transfers between devices, partner(): return lax.ppermute(x, 'right', [(i, i ^ step) for i in range(4)])  37.2 us
    ppermute x5, starting transfers between devices, hop(): return lax.ppermute(x, 'left', pairs)  13.8 us
    pallas_call x1, Pallas kernels, early_sums(): pl.pallas_call(functools.partial(early_kernel, places), out_shape=[jax.Sh...  11.4 us
    pallas_call x2, Pallas kernels, pair_features(): pl.pallas_call(functools.partial(late_kernel, line, start), out_shape=jax...  6.92 us
    ppermute x5, waiting for transfers between devices, hop(): return lax.ppermute(x, 'left', pairs)  5.35 us
    ppermute x5, starting transfers between devices, partner(): return lax.ppermute(x, 'right', [(i, i ^ step) for i in range(4)])  3.67 us
  transfers between devices with their start and end apart: 10, of which 3 were waited for; matrix products, arithmetic and copies ran while one was open for 7% of the time, Pallas kernels for 18%

profile of v4, /device:TPU:0, one launch (start us, length us, event | category | flops | bytes accessed | tf_op | source)
XLA Modules:
  0.0 84.2 jit_solution(17735979476578486301)
XLA Ops:
  0.0 3.0 %collective-permute-start.1 = (bf16[512,2048]{1,0:T(8,128)(2,1)}, bf16[512,2048]{1,0:T(8,128)(2,1)S(1)}, u32[]{:S(2)}, u32[]{:S(2)}) collective-permute-start(bf16[512,2048]{1,0:T(8,128)(2,1)} %refs_0_.1), channel_id=1, source_target_pairs={{0,8},{4,12},{8,0},{12,4},{1,9},{5,13},{9,1},{13,5},{2,10},{6,14},... | collective-permute-start | bytes 6291464 | tf_op jit(solution)/shard_map/ppermute | solution.py:191
  3.0 1.6 %collective-permute-start.5 = (bf16[512,1024]{1,0:T(8,128)(2,1)}, bf16[512,1024]{1,0:T(8,128)(2,1)}, u32[]{:S(2)}, u32[]{:S(2)}) collective-permute-start(bf16[512,1024]{1,0:T(8,128)(2,1)} %refs_6_.1), channel_id=1, source_target_pairs={{0,1},{1,0},{2,3},{3,2},{4,5},{5,4},{6,7},{7,6},{8,9},{9,8},{10,11... | collective-permute-start | bytes 3145736 | tf_op jit(solution)/shard_map/ppermute | solution.py:188
  4.5 0.7 collective-permute-start.6
  5.3 4.4 %collective-permute-start.7 = (bf16[512,1024]{1,0:T(8,128)(2,1)}, bf16[512,1024]{1,0:T(8,128)(2,1)}, u32[]{:S(2)}, u32[]{:S(2)}) collective-permute-start(bf16[512,1024]{1,0:T(8,128)(2,1)} %refs_6_.1), channel_id=1, source_target_pairs={{0,3},{3,0},{4,7},{7,4},{8,11},{11,8},{12,15},{15,12},{16,19},{19,... | collective-permute-start | bytes 3145736 | tf_op jit(solution)/shard_map/ppermute | solution.py:188
  9.7 1.1 %copy.6 = bf16[32,32,128]{2,1,0:T(8,128)(2,1)S(1)} copy(bf16[32,32,128]{2,0,1:T(8,128)(2,1)} %bitcast.18) | data formatting | bytes 524288 | tf_op jit(solution)/shard_map/transpose | solution.py:23
  10.8 0.0 copy-start
  10.8 1.6 %broadcast_select_fusion = bf16[32,4,32,4,128]{4,3,2,1,0:T(4,128)(2,1)S(1)} fusion(pred[4,4]{1,0:T(4,128)(4,1)S(1)} %iota_compare_fusion, bf16[32,32,128]{2,1,0:T(8,128)(2,1)S(1)} %copy.6), kind=kLoop, calls=%fused_computation.1 | loop fusion | flops 2097152 | bytes 4456464 | tf_op jit(solution)/shard_map/jit(_where)/select_n | solution.py:25
  12.4 36.4 %collective-permute-done.1.refs_2_ = bf16[512,2048]{1,0:T(8,128)(2,1)S(1)} collective-permute-done((bf16[512,2048]{1,0:T(8,128)(2,1)}, bf16[512,2048]{1,0:T(8,128)(2,1)S(1)}, u32[]{:S(2)}, u32[]{:S(2)}) %collective-permute-start.1) | collective-permute-done | bytes 2097184 | tf_op jit(solution)/shard_map/ppermute | solution.py:191
  48.8 0.1 slice.45
  48.9 0.1 collective-permute-start.2
  49.0 0.4 compare_and_fusion
  49.4 0.1 slice.46
  49.4 0.6 collective-permute-start.3
  50.0 1.5 %and_select_fusion = (bf16[512,512]{1,0:T(8,128)(2,1)S(1)}, bf16[512,512]{1,0:T(8,128)(2,1)S(1)}) fusion(bf16[512,1024]{1,0:T(8,128)(2,1)S(1)} %collective-permute-done.6.refs_8_, bf16[512,1024]{1,0:T(8,128)(2,1)} %collective-permute-done.5.refs_7_, bf16[512,1024]{1,0:T(8,128)(2,1)S(1)} %copy-done, pred[]{:T(512)S(6)} %eq.19, ...), kind=kLoop, calls=%fused_computation.3 | loop fusion | flops 1310720 | bytes 3932161 | tf_op jit(solution)/shard_map/jit(_where)/select_n | solution.py:198
  51.5 7.0 %collective-permute-start.9 = (bf16[512,512]{1,0:T(8,128)(2,1)S(1)}, bf16[512,512]{1,0:T(8,128)(2,1)S(1)}, u32[]{:S(2)}, u32[]{:S(2)}) collective-permute-start(bf16[512,512]{1,0:T(8,128)(2,1)S(1)} %get-tuple-element.11), channel_id=1, source_target_pairs={{0,2},{3,1},{1,0},{2,3},{4,6},{7,5},{5,4},{6,7},{8,10},{11,9},{9,8... | collective-permute-start | bytes 1572872 | tf_op jit(solution)/shard_map/ppermute | solution.py:188
  58.6 0.1 collective-permute-start.8
  58.7 0.1 collective-permute-start.4
  58.8 0.7 copy.11
  59.6 0.7 collective-permute-done.4.refs_5_
  60.3 0.1 copy-done.1
  60.4 11.4 %shard_map.46 = (f32[512,2048]{1,0:T(8,128)S(1)}, f32[512,2048]{1,0:T(8,128)S(1)}, bf16[512,2048]{1,0:T(8,128)(2,1)S(1)}) custom-call(bf16[512,2048]{1,0:T(8,128)(2,1)S(1)} %copy-done.1, bf16[512,2048]{1,0:T(8,128)(2,1)} %collective-permute-done.refs_1_, bf16[512,2048]{1,0:T(8,128)(2,1)S(1)} %collective-permute-done.1.refs_2_, ...), custom_call_target="tpu_custom_call" | custom-call | flops 1 | bytes 1 | tf_op jit(solution)/shard_map/pallas_call | solution.py:105
  71.8 3.5 %shard_map.47.refs_5_ = f32[64,32,128]{2,1,0:T(8,128)} custom-call(f32[512,2048]{1,0:T(8,128)S(1)} %get-tuple-element.10.refs_0_, bf16[512,2048]{1,0:T(8,128)(2,1)S(1)} %get-tuple-element.9.refs_1_, bf16[512,512]{1,0:T(8,128)(2,1)S(1)} %collective-permute-done.9.refs_2_, bf16[4096,512]{1,0:T(8,128)(2,1)S(1)} %bitcast.14, f32[16,64]{1,0:T(8,128)S(1)} %get-tuple-element.13.refs_4_), custom_call_target="tpu_custom_call" | custom-call | flops 1 | bytes 1 | tf_op jit(solution)/shard_map/pallas_call | solution.py:166
  75.2 5.3 %collective-permute-done.8.refs_2_ = bf16[512,512]{1,0:T(8,128)(2,1)S(1)} collective-permute-done((bf16[512,512]{1,0:T(8,128)(2,1)S(1)}, bf16[512,512]{1,0:T(8,128)(2,1)S(1)}, u32[]{:S(2)}, u32[]{:S(2)}) %collective-permute-start.8) | collective-permute-done | bytes 524320 | tf_op jit(solution)/shard_map/ppermute | solution.py:188
  80.6 3.5 %shard_map.48 = f32[64,32,128]{2,1,0:T(8,128)} custom-call(f32[512,2048]{1,0:T(8,128)S(1)} %get-tuple-element.8.refs_0_, bf16[512,2048]{1,0:T(8,128)(2,1)S(1)} %get-tuple-element.9.refs_1_, bf16[512,512]{1,0:T(8,128)(2,1)S(1)} %collective-permute-done.8.refs_2_, bf16[4096,512]{1,0:T(8,128)(2,1)S(1)} %bitcast.15, ...), custom_call_target="tpu_custom_call", output_to_operand_aliasing={{}: (5, {})} | custom-call | flops 1 | bytes 1 | tf_op jit(solution)/shard_map/pallas_call | solution.py:166
  (16 shorter events, 0.1 us)
Async XLA Ops:
  0.0 48.8 %collective-permute-start.1 = (bf16[512,2048]{1,0:T(8,128)(2,1)}, bf16[512,2048]{1,0:T(8,128)(2,1)S(1)}, u32[]{:S(2)}, u32[]{:S(2)}) collective-permute-start(bf16[512,2048]{1,0:T(8,128)(2,1)} %refs_0_.1), channel_id=1, source_target_pairs={{0,8},{4,12},{8,0},{12,4},{1,9},{5,13},{9,1},{13,5},{2,10},{6,14},... | collective-permute-start | bytes 6291464 | tf_op jit(solution)/shard_map/ppermute | solution.py:191
  3.0 55.7 %collective-permute-start = (bf16[512,2048]{1,0:T(8,128)(2,1)}, bf16[512,2048]{1,0:T(8,128)(2,1)}, u32[]{:S(2)}, u32[]{:S(2)}) collective-permute-start(bf16[512,2048]{1,0:T(8,128)(2,1)} %refs_0_.1), channel_id=1, source_target_pairs={{0,4},{4,0},{8,12},{12,8},{1,5},{5,1},{9,13},{13,9},{2,6},{6,2},{1... | collective-permute-start | bytes 6291464 | tf_op jit(solution)/shard_map/ppermute | solution.py:191
  3.0 46.5 %collective-permute-start.5 = (bf16[512,1024]{1,0:T(8,128)(2,1)}, bf16[512,1024]{1,0:T(8,128)(2,1)}, u32[]{:S(2)}, u32[]{:S(2)}) collective-permute-start(bf16[512,1024]{1,0:T(8,128)(2,1)} %refs_6_.1), channel_id=1, source_target_pairs={{0,1},{1,0},{2,3},{3,2},{4,5},{5,4},{6,7},{7,6},{8,9},{9,8},{10,11... | collective-permute-start | bytes 3145736 | tf_op jit(solution)/shard_map/ppermute | solution.py:188
  4.5 45.5 %collective-permute-start.6 = (bf16[512,1024]{1,0:T(8,128)(2,1)}, bf16[512,1024]{1,0:T(8,128)(2,1)S(1)}, u32[]{:S(2)}, u32[]{:S(2)}) collective-permute-start(bf16[512,1024]{1,0:T(8,128)(2,1)} %refs_6_.1), channel_id=1, source_target_pairs={{1,2},{2,1},{5,6},{6,5},{9,10},{10,9},{13,14},{14,13},{17,18},{18,... | collective-permute-start | bytes 3145736 | tf_op jit(solution)/shard_map/ppermute | solution.py:188
  5.3 53.3 %collective-permute-start.7 = (bf16[512,1024]{1,0:T(8,128)(2,1)}, bf16[512,1024]{1,0:T(8,128)(2,1)}, u32[]{:S(2)}, u32[]{:S(2)}) collective-permute-start(bf16[512,1024]{1,0:T(8,128)(2,1)} %refs_6_.1), channel_id=1, source_target_pairs={{0,3},{3,0},{4,7},{7,4},{8,11},{11,8},{12,15},{15,12},{16,19},{19,... | collective-permute-start | bytes 3145736 | tf_op jit(solution)/shard_map/ppermute | solution.py:188
  10.8 39.3 %copy-start = (bf16[512,1024]{1,0:T(8,128)(2,1)S(1)}, bf16[512,1024]{1,0:T(8,128)(2,1)}, u32[]{:S(2)}) copy-start(bf16[512,1024]{1,0:T(8,128)(2,1)} %refs_6_.1) | copy-start | bytes 3145732
  12.4 46.4 %copy-start.2 = (s32[64,32]{0,1:T(8,128)S(1)}, s32[64,32]{0,1:T(8,128)}, u32[]{:S(2)}) copy-start(s32[64,32]{0,1:T(8,128)} %param.6) | copy-start | bytes 24580
  48.9 11.4 %collective-permute-start.2 = (bf16[256,2048]{1,0:T(8,128)(2,1)S(1)}, bf16[256,2048]{1,0:T(8,128)(2,1)S(1)}, u32[]{:S(2)}, u32[]{:S(2)}) collective-permute-start(bf16[256,2048]{1,0:T(8,128)(2,1)S(1)} %slice.45), channel_id=1, source_target_pairs={{0,4},{4,0},{8,12},{12,8},{1,5},{5,1},{9,13},{13,9},{2,6},{6,2},{1... | collective-permute-start | bytes 3145736 | tf_op jit(solution)/shard_map/ppermute | solution.py:191
  49.4 10.9 %collective-permute-start.3 = (bf16[192,2048]{1,0:T(8,128)(2,1)S(1)}, bf16[192,2048]{1,0:T(8,128)(2,1)S(1)}, u32[]{:S(2)}, u32[]{:S(2)}) collective-permute-start(bf16[192,2048]{1,0:T(8,128)(2,1)S(1)} %slice.46), channel_id=1, source_target_pairs={{0,4},{4,0},{8,12},{12,8},{1,5},{5,1},{9,13},{13,9},{2,6},{6,2},{1... | collective-permute-start | bytes 2359304 | tf_op jit(solution)/shard_map/ppermute | solution.py:191
  51.5 20.2 %collective-permute-start.9 = (bf16[512,512]{1,0:T(8,128)(2,1)S(1)}, bf16[512,512]{1,0:T(8,128)(2,1)S(1)}, u32[]{:S(2)}, u32[]{:S(2)}) collective-permute-start(bf16[512,512]{1,0:T(8,128)(2,1)S(1)} %get-tuple-element.11), channel_id=1, source_target_pairs={{0,2},{3,1},{1,0},{2,3},{4,6},{7,5},{5,4},{6,7},{8,10},{11,9},{9,8... | collective-permute-start | bytes 1572872 | tf_op jit(solution)/shard_map/ppermute | solution.py:188
  58.6 22.0 %collective-permute-start.8 = (bf16[512,512]{1,0:T(8,128)(2,1)S(1)}, bf16[512,512]{1,0:T(8,128)(2,1)S(1)}, u32[]{:S(2)}, u32[]{:S(2)}) collective-permute-start(bf16[512,512]{1,0:T(8,128)(2,1)S(1)} %get-tuple-element.12), channel_id=1, source_target_pairs={{0,2},{3,1},{1,0},{2,3},{4,6},{7,5},{5,4},{6,7},{8,10},{11,9},{9,8... | collective-permute-start | bytes 1572872 | tf_op jit(solution)/shard_map/ppermute | solution.py:188
  58.7 1.6 %collective-permute-start.4 = (bf16[64,2048]{1,0:T(8,128)(2,1)S(1)}, bf16[64,2048]{1,0:T(8,128)(2,1)S(1)}, u32[]{:S(2)}, u32[]{:S(2)}) collective-permute-start(bf16[64,2048]{1,0:T(8,128)(2,1)S(1)} %slice.47), channel_id=1, source_target_pairs={{0,4},{4,0},{8,12},{12,8},{1,5},{5,1},{9,13},{13,9},{2,6},{6,2},{1... | collective-permute-start | bytes 786440 | tf_op jit(solution)/shard_map/ppermute | solution.py:191
  58.8 1.6 %copy-start.1 = (bf16[512,2048]{1,0:T(8,128)(2,1)S(1)}, bf16[512,2048]{1,0:T(8,128)(2,1)}, u32[]{:S(2)}) copy-start(bf16[512,2048]{1,0:T(8,128)(2,1)} %refs_0_.1) | copy-start | bytes 6291460
